TPU v7x, 32 devices: a whole 2x2x4 slice. The times are simulated.
32 devices in a mesh: loop: 4 (over y, x), grp: 8 (over z, core).
Axes of the slice: x: 2, y: 2, z: 4, core: 2. Of those that a mesh axis runs over, the one named last changes fastest.
Arguments:
- queries: bfloat16 [4096, 4096], P(('loop', 'grp')), as said below
- passages: bfloat16 [2048, 4096], P(('loop', 'grp')), as said below
- pool: bfloat16 [8192, 4096], P(('loop', 'grp')), as said below
- query_count: int32 [4, 8], P('loop', 'grp'), may hold values from 32 to 128, as said below
- positive: int32 [4096], P(('loop', 'grp')), may hold values from 0 to 255
- neg_owner: int32 [4096, 7], P(('loop', 'grp')), may hold values from 0 to 7, as said below
- neg_row: int32 [4096, 7], P(('loop', 'grp')), may hold values from 0 to 255
Outputs:
- loss: float32 [4096], P(('loop', 'grp'))
- grad_query: float32 [4096, 4096], P(('loop', 'grp'))
- grad_passage: float32 [2048, 4096], P(('loop', 'grp'))
- grad_pool: float32 [8192, 4096], P(('loop', 'grp'))
Inputs may be any that keep to these rules, and one draw needn't show every extreme that they name: `queries`: every entry lies in -0.25 to 0.25. `passages`: every entry lies in -0.25 to 0.25. `pool`: every entry lies in -0.25 to 0.25. `query_count`: some device has all 128 slots live. `neg_owner`: among the 896 entries of one device, at most 140 name one owner; for every loop index one owner is named exactly 140 times by every device of that loop index. Entries of slots that are not live are present too.
All inputs are finite; a program needn't handle non-finite values.
Results may differ from a plain program's by a relative error of at most 0.02.
Values may be sent and summed in bfloat16 or wider, within the bound.
A program may use at most 192 MiB of HBM per device.

v0:
```python
import jax
import jax.numpy as jnp
from jax import lax
from jax.sharding import PartitionSpec as P

inv_temp = 50.0
eps = 1e-06


def passed_along(shard, axis, by):
    peers = lax.axis_size(axis)
    return lax.ppermute(shard, axis, [(i, (i + by) % peers) for i in range(peers)])


def unit_rows(rows):
    scale = lax.rsqrt(jnp.sum(rows * rows, axis=-1, keepdims=True) + eps)
    return (rows * scale, scale)


def unit_back(grad, unit, scale):
    return (grad - unit * jnp.sum(unit * grad, axis=-1, keepdims=True)) * scale


def cross(left, right):
    return lax.dot_general(
        left, right, (((1,), (1,)), ((), ())), preferred_element_type=jnp.float32
    )


def gather_back(coef, rows):
    return lax.dot_general(coef, rows, (((0,), (0,)), ((), ())), preferred_element_type=jnp.float32)


def local(queries, passages, pool, query_count, positive, neg_owner, neg_row):
    n_query, width = queries.shape
    n_pass = passages.shape[0]
    hard_count = neg_owner.shape[1]
    groups = lax.axis_size("grp")
    loops = lax.axis_size("loop")
    blocks_total = loops * n_pass
    cap = 5 * n_query * hard_count // (4 * groups)
    q_unit, q_scale = unit_rows(queries.astype(jnp.float32))
    p_unit, p_scale = unit_rows(passages.astype(jnp.float32))
    n_unit, n_scale = unit_rows(pool.astype(jnp.float32))
    q_hat = q_unit.astype(jnp.bfloat16)
    p_hat = p_unit.astype(jnp.bfloat16)
    n_hat = n_unit.astype(jnp.bfloat16)
    valid = (lax.iota(jnp.int32, n_query) < query_count.reshape(())).astype(jnp.float32)[:, None]
    owners = neg_owner.reshape(-1)
    wanted_rows = neg_row.reshape(-1)
    owner_hits = (owners[:, None] == lax.iota(jnp.int32, groups)[None, :]).astype(jnp.int32)
    rank = jnp.sum((jnp.cumsum(owner_hits, axis=0) - owner_hits) * owner_hits, axis=1)
    place = owners * cap + rank
    send_ids = jnp.zeros((groups * cap,), jnp.int32).at[place].set(wanted_rows).reshape(groups, cap)
    requested = lax.all_to_all(send_ids, "grp", split_axis=0, concat_axis=0, tiled=True)
    picked = n_hat[requested]
    reply = lax.all_to_all(picked, "grp", split_axis=0, concat_axis=0, tiled=True)
    negs = reply.reshape(groups * cap, width)[place].reshape(n_query, hard_count, width)
    hard = jnp.einsum("qd,qkd->qk", q_hat, negs, preferred_element_type=jnp.float32) * inv_temp
    scores = cross(q_hat, lax.all_gather(p_hat, "loop", axis=0, tiled=True)) * inv_temp
    weights_in = jnp.exp(scores - inv_temp)
    weights_hard = jnp.exp(hard - inv_temp)
    total = jnp.sum(weights_in, axis=1) + jnp.sum(weights_hard, axis=1)
    chosen = jnp.take_along_axis(scores, positive[:, None], axis=1)[:, 0]
    loss = valid[:, 0] * (jnp.log(total) + inv_temp - chosen)
    target = (positive[:, None] == lax.iota(jnp.int32, blocks_total)[None, :]).astype(jnp.float32)
    coef_in = (valid * (weights_in / total[:, None] - target)).astype(jnp.bfloat16)
    coef_hard = (valid * weights_hard / total[:, None]).astype(jnp.bfloat16)
    hard_part = jnp.einsum("qk,qkd->qd", coef_hard, negs, preferred_element_type=jnp.float32)
    neg_grad = (
        inv_temp * coef_hard.astype(jnp.float32)[:, :, None] * q_hat.astype(jnp.float32)[:, None, :]
    ).astype(jnp.bfloat16)
    position = lax.axis_index("loop")

    def turn(step, carry):
        block, block_sum, query_sum = carry
        anchor = (position - step) % loops
        cols = lax.dynamic_slice_in_dim(coef_in, anchor * n_pass, n_pass, 1)
        query_sum = query_sum + jnp.dot(cols, block, preferred_element_type=jnp.float32)
        block_sum = block_sum + gather_back(cols, q_hat)
        block, block_sum = (
            passed_along(block, "loop", 1),
            passed_along(block_sum.astype(jnp.bfloat16), "loop", 1).astype(block_sum.dtype),
        )
        return (block, block_sum, query_sum)

    start_carry = (
        p_hat,
        jnp.zeros((n_pass, width), jnp.float32),
        jnp.zeros((n_query, width), jnp.float32),
    )
    unused, pass_part, in_part = lax.fori_loop(0, loops, turn, start_carry)
    grad_query = unit_back(inv_temp * (in_part + hard_part), q_unit, q_scale)
    grad_passage = unit_back(inv_temp * pass_part, p_unit, p_scale)
    outgoing = (
        jnp.zeros((groups * cap, width), jnp.bfloat16).at[place].set(neg_grad.reshape(-1, width))
    )
    incoming = lax.all_to_all(
        outgoing.reshape(groups, cap, width), "grp", split_axis=0, concat_axis=0, tiled=True
    )
    pool_sum = jax.ops.segment_sum(
        incoming.reshape(-1, width).astype(jnp.float32),
        requested.reshape(-1),
        num_segments=pool.shape[0],
    )
    grad_pool = unit_back(pool_sum, n_unit, n_scale)
    return (loss, grad_query, grad_passage, grad_pool)


def solution(mesh):
    return jax.shard_map(
        local,
        mesh=mesh,
        in_specs=(
            P(("loop", "grp"), None),
            P(("loop", "grp"), None),
            P(("loop", "grp"), None),
            P("loop", "grp"),
            P(("loop", "grp")),
            P(("loop", "grp"), None),
            P(("loop", "grp"), None),
        ),
        out_specs=(
            P(("loop", "grp")),
            P(("loop", "grp"), None),
            P(("loop", "grp"), None),
            P(("loop", "grp"), None),
        ),
        check_vma=False,
    )
```

profile of v0, /device:TPU:10, one launch (start us, length us, event | category | flops | bytes accessed | tf_op | source)
XLA Modules:
  0.0 621.2 jit_solution(12384393983665153257)
XLA Ops:
  28.7 7.9 %gather_fusion = bf16[1120,4096]{1,0:T(8,128)(2,1)} fusion(bf16[256,4096]{1,0:T(8,128)(2,1)S(1)} %fusion.8, s32[2048]{0:T(1024)S(1)} %pad_clamp_fusion), kind=kCustom, calls=%fused_computation | custom fusion | bytes 18354560 | tf_op jit(solution)/shard_map/gather | solution.py:56
  36.6 8.1 %reshape.175 = bf16[8,140,4096]{2,1,0:T(8,128)(2,1)} reshape(bf16[1120,4096]{1,0:T(8,128)(2,1)} %gather_fusion) | data formatting | bytes 18350080 | tf_op jit(solution)/shard_map/gather | solution.py:56
  54.0 7.9 %mul.208 = f32[128,7,4096]{2,1,0:T(8,128)} broadcast(bf16[128,4096]{1,0:T(8,128)(2,1)S(1)} %fusion.16), dimensions={0,2} | broadcast | bytes 15728640 | tf_op jit(solution)/shard_map/mul | solution.py:71
  61.9 13.7 %mul.209 = f32[896,4096]{1,0:T(8,128)} reshape(f32[128,7,4096]{2,1,0:T(8,128)} %mul.208) | data formatting | bytes 29360128 | tf_op jit(solution)/shard_map/mul | solution.py:71
  76.9 13.1 %all-gather.2.cloned.1.call-done = bf16[256,4096]{1,0:T(8,128)(2,1)} async-done(((bf16[64,4096]{1,0:T(8,128)(2,1)}), bf16[256,4096]{1,0:T(8,128)(2,1)}) %all-gather.2.cloned.1.call-update) | async-done | bytes 2097168 | tf_op jit(solution)/shard_map/all_gather | solution.py:60
  94.0 159.9 %all-to-all-done.1 = bf16[8,140,4096]{2,1,0:T(8,128)(2,1)} async-done(((bf16[8,140,4096]{2,1,0:T(8,128)(2,1)}), bf16[8,140,4096]{2,1,0:T(8,128)(2,1)}, u32[]{:S(2)}, u32[]{:S(2)}) %all-to-all-start.1) | async-done | bytes 9175072 | tf_op jit(solution)/shard_map/all_to_all | solution.py:57
  253.9 8.1 %reshape.169 = bf16[1120,4096]{1,0:T(8,128)(2,1)} reshape(bf16[8,140,4096]{2,1,0:T(8,128)(2,1)} %all-to-all-done.1) | data formatting | bytes 18350080 | tf_op jit(solution)/shard_map/reshape | solution.py:58
  262.0 19.8 %gather_fusion.1 = bf16[896,4096]{1,0:T(8,128)(2,1)} fusion(bf16[1120,4096]{1,0:T(8,128)(2,1)} %reshape.169, s32[1024]{0:T(1024)S(1)} %pad_clamp_fusion.1), kind=kCustom, calls=%fused_computation.1 | custom fusion | bytes 14683648 | tf_op jit(solution)/shard_map/gather | solution.py:58
  281.8 9.6 %reshape.170 = bf16[128,7,4096]{2,1,0:T(8,128)(2,1)} reshape(bf16[896,4096]{1,0:T(8,128)(2,1)} %gather_fusion.1) | data formatting | bytes 14680064 | tf_op jit(solution)/shard_map/reshape | solution.py:58
  291.5 8.8 %fusion.22 = f32[128,1,7]{2,1,0:T(1,128)S(1)} fusion(bf16[128,7,4096]{2,1,0:T(8,128)(2,1)} %reshape.170, bf16[128,4096,1]{1,0,2:T(8,128)(2,1)S(1)} %copy-done.7), kind=kOutput, calls=%fused_computation.36 | convolution fusion | flops 7340032 | bytes 8392192 | tf_op jit(solution)/shard_map/qd,qkd->qk/dot_general | solution.py:59
  307.5 22.8 %scatter_custom_fusion.1 = bf16[1120,4096]{1,0:T(8,128)(2,1)} fusion(s32[896]{0:T(1024)S(1)} %fusion.42, f32[896,4096]{1,0:T(8,128)} %mul.207, f32[896,4096]{1,0:T(8,128)} %mul.209, bf16[]{:T(256)} %constant.118.clone.1), kind=kCustom, calls=%fused_computation.14 | custom fusion | flops 7340032 | bytes 38535168 | tf_op jit(solution)/shard_map/scatter | solution.py:96
  330.3 8.1 %reshape.172 = bf16[8,140,4096]{2,1,0:T(8,128)(2,1)} reshape(bf16[1120,4096]{1,0:T(8,128)(2,1)} %scatter_custom_fusion.1) | data formatting | bytes 18350080 | tf_op jit(solution)/shard_map/reshape | solution.py:99
  338.5 8.5 %all-to-all-start.2 = ((bf16[8,140,4096]{2,1,0:T(8,128)(2,1)}), bf16[8,140,4096]{2,1,0:T(8,128)(2,1)}, u32[]{:S(2)}, u32[]{:S(2)}) async-start(bf16[8,140,4096]{2,1,0:T(8,128)(2,1)} %reshape.172), calls=%async_computation.2 | async-start | bytes 18874368 | tf_op jit(solution)/shard_map/all_to_all | solution.py:98
  347.4 107.1 %while.20 = (s32[]{:T(128)}, bf16[64,4096]{1,0:T(8,128)(2,1)}, f32[64,4096]{1,0:T(8,128)}, f32[128,4096]{1,0:T(8,128)S(1)}, s32[]{:T(128)}, /*index=5*/bf16[128,...) while((s32[]{:T(128)}, bf16[64,4096]{1,0:T(8,128)(2,1)}, ...), condition=%wide.region_10.11_spmd.clone, body=%wide.region_9.10_spmd.clone.sunk | while | flops 136314896 | bytes 14221703 | solution.py:92
  355.3 8.4 %collective-permute-done.1 = bf16[64,4096]{1,0:T(8,128)(2,1)} collective-permute-done((bf16[64,4096]{1,0:T(8,128)(2,1)}, bf16[64,4096]{1,0:T(8,128)(2,1)}, u32[]{:S(2)}, u32[]{:S(2)}) %collective-permute-start.1) | collective-permute-done | bytes 524320 | tf_op jit(solution)/shard_map/while/body/eval_jaxpr/ppermute | solution.py:12
  365.8 8.4 %collective-permute-done = bf16[64,4096]{1,0:T(8,128)(2,1)} collective-permute-done((bf16[64,4096]{1,0:T(8,128)(2,1)}, bf16[64,4096]{1,0:T(8,128)(2,1)}, u32[]{:S(2)}, u32[]{:S(2)}) %collective-permute-start) | collective-permute-done | bytes 524320 | tf_op jit(solution)/shard_map/while/body/eval_jaxpr/ppermute | solution.py:12
  383.3 8.5 %collective-permute-done.1 = bf16[64,4096]{1,0:T(8,128)(2,1)} collective-permute-done((bf16[64,4096]{1,0:T(8,128)(2,1)}, bf16[64,4096]{1,0:T(8,128)(2,1)}, u32[]{:S(2)}, u32[]{:S(2)}) %collective-permute-start.1) | collective-permute-done | bytes 524320 | tf_op jit(solution)/shard_map/while/body/eval_jaxpr/ppermute | solution.py:12
  393.8 7.4 %collective-permute-done = bf16[64,4096]{1,0:T(8,128)(2,1)} collective-permute-done((bf16[64,4096]{1,0:T(8,128)(2,1)}, bf16[64,4096]{1,0:T(8,128)(2,1)}, u32[]{:S(2)}, u32[]{:S(2)}) %collective-permute-start) | collective-permute-done | bytes 524320 | tf_op jit(solution)/shard_map/while/body/eval_jaxpr/ppermute | solution.py:12
  410.7 9.0 %collective-permute-done.1 = bf16[64,4096]{1,0:T(8,128)(2,1)} collective-permute-done((bf16[64,4096]{1,0:T(8,128)(2,1)}, bf16[64,4096]{1,0:T(8,128)(2,1)}, u32[]{:S(2)}, u32[]{:S(2)}) %collective-permute-start.1) | collective-permute-done | bytes 524320 | tf_op jit(solution)/shard_map/while/body/eval_jaxpr/ppermute | solution.py:12
  421.8 6.5 %collective-permute-done = bf16[64,4096]{1,0:T(8,128)(2,1)} collective-permute-done((bf16[64,4096]{1,0:T(8,128)(2,1)}, bf16[64,4096]{1,0:T(8,128)(2,1)}, u32[]{:S(2)}, u32[]{:S(2)}) %collective-permute-start) | collective-permute-done | bytes 524320 | tf_op jit(solution)/shard_map/while/body/eval_jaxpr/ppermute | solution.py:12
  437.9 9.0 %collective-permute-done.1 = bf16[64,4096]{1,0:T(8,128)(2,1)} collective-permute-done((bf16[64,4096]{1,0:T(8,128)(2,1)}, bf16[64,4096]{1,0:T(8,128)(2,1)}, u32[]{:S(2)}, u32[]{:S(2)}) %collective-permute-start.1) | collective-permute-done | bytes 524320 | tf_op jit(solution)/shard_map/while/body/eval_jaxpr/ppermute | solution.py:12
  468.4 81.5 %all-to-all-done.2 = bf16[8,140,4096]{2,1,0:T(8,128)(2,1)} async-done(((bf16[8,140,4096]{2,1,0:T(8,128)(2,1)}), bf16[8,140,4096]{2,1,0:T(8,128)(2,1)}, u32[]{:S(2)}, u32[]{:S(2)}) %all-to-all-start.2) | async-done | bytes 9175072 | tf_op jit(solution)/shard_map/all_to_all | solution.py:98
  549.9 16.9 %reshape.218 = f32[1120,4096]{1,0:T(8,128)} reshape(bf16[8,140,4096]{2,1,0:T(8,128)(2,1)} %all-to-all-done.2) | data formatting | bytes 27525120 | tf_op jit(solution)/shard_map/convert_element_type | solution.py:102
  566.7 40.9 %scatter_custom_fusion.2 = f32[256,4096]{1,0:T(8,128)} fusion(s32[1120]{0:T(1024)S(1)} %reshape.216, f32[1120,4096]{1,0:T(8,128)} %reshape.218, f32[]{:T(128)} %constant.107.clone.1), kind=kCustom, calls=%fused_computation.38 | custom fusion | flops 4587520 | bytes 4194816 | tf_op jit(solution)/shard_map/scatter-add | solution.py:101
  (107 shorter events, 113.2 us)
Async XLA Ops:
  18.9 9.6 %all-to-all-start = ((s32[8,1,140]{2,1,0:T(1,128)}), s32[8,1,140]{2,1,0:T(1,128)S(1)}, u32[]{:S(2)}, u32[]{:S(2)}) async-start(s32[8,1,140]{2,1,0:T(1,128)} %all_to_all.14), calls=%async_computation | async-start | bytes 16384 | tf_op jit(solution)/shard_map/all_to_all | solution.py:55
  44.7 6.9 %copy-start.5 = (bf16[64,4096]{1,0:T(8,128)(2,1)S(1)}, bf16[64,4096]{1,0:T(8,128)(2,1)}, u32[]{:S(2)}) copy-start(bf16[64,4096]{1,0:T(8,128)(2,1)} %param.10) | copy-start | bytes 1572868
  44.7 8.7 %copy-start.3 = (bf16[128,4096]{1,0:T(8,128)(2,1)S(1)}, bf16[128,4096]{1,0:T(8,128)(2,1)}, u32[]{:S(2)}) copy-start(bf16[128,4096]{1,0:T(8,128)(2,1)} %param.9) | copy-start | bytes 3145732
  44.7 209.3 %all-to-all-start.1 = ((bf16[8,140,4096]{2,1,0:T(8,128)(2,1)}), bf16[8,140,4096]{2,1,0:T(8,128)(2,1)}, u32[]{:S(2)}, u32[]{:S(2)}) async-start(bf16[8,140,4096]{2,1,0:T(8,128)(2,1)} %reshape.175), calls=%async_computation.1 | async-start | bytes 18874368 | tf_op jit(solution)/shard_map/all_to_all | solution.py:57
  51.1 39.0 %all-gather.2.cloned.1.call-start = ((), (), s32[]{:S(2)}) async-start(), calls=%async_computation.3 | async-start | bytes 2621440 | tf_op jit(solution)/shard_map/all_gather | solution.py:60
  61.9 13.7 %copy-start.8 = (s32[128]{0:T(128)S(1)}, s32[128]{0:T(128)}, u32[]{:S(2)}) copy-start(s32[128]{0:T(128)} %param.13) | copy-start | bytes 1540
  281.8 9.6 %copy-start.7 = (bf16[128,4096,1]{1,0,2:T(8,128)(2,1)S(1)}, bf16[128,4096,1]{1,0,2:T(8,128)(2,1)}, u32[]{:S(2)}) copy-start(bf16[128,4096,1]{1,0,2:T(8,128)(2,1)} %fusion.54) | copy-start | bytes 3145732
  338.5 211.4 %all-to-all-start.2 = ((bf16[8,140,4096]{2,1,0:T(8,128)(2,1)}), bf16[8,140,4096]{2,1,0:T(8,128)(2,1)}, u32[]{:S(2)}, u32[]{:S(2)}) async-start(bf16[8,140,4096]{2,1,0:T(8,128)(2,1)} %reshape.172), calls=%async_computation.2 | async-start | bytes 18874368 | tf_op jit(solution)/shard_map/all_to_all | solution.py:98
  348.6 15.1 %collective-permute-start.1 = (bf16[64,4096]{1,0:T(8,128)(2,1)}, bf16[64,4096]{1,0:T(8,128)(2,1)}, u32[]{:S(2)}, u32[]{:S(2)}) collective-permute-start(bf16[64,4096]{1,0:T(8,128)(2,1)} %fusion.64), channel_id=1, source_target_pairs={{0,8},{8,16},{16,24},{24,0},{1,9},{9,17},{17,25},{25,1},{2,10},{10... | collective-permute-start | bytes 1572872 | tf_op jit(solution)/shard_map/while/body/eval_jaxpr/ppermute | solution.py:12
  352.0 22.2 %collective-permute-start = (bf16[64,4096]{1,0:T(8,128)(2,1)}, bf16[64,4096]{1,0:T(8,128)(2,1)}, u32[]{:S(2)}, u32[]{:S(2)}) collective-permute-start(bf16[64,4096]{1,0:T(8,128)(2,1)} %copy.42), channel_id=1, source_target_pairs={{0,8},{8,16},{16,24},{24,0},{1,9},{9,17},{17,25},{25,1},{2,10},{10... | collective-permute-start | bytes 1572872 | tf_op jit(solution)/shard_map/while/body/eval_jaxpr/ppermute | solution.py:12
  376.6 15.2 %collective-permute-start.1 = (bf16[64,4096]{1,0:T(8,128)(2,1)}, bf16[64,4096]{1,0:T(8,128)(2,1)}, u32[]{:S(2)}, u32[]{:S(2)}) collective-permute-start(bf16[64,4096]{1,0:T(8,128)(2,1)} %fusion.64), channel_id=1, source_target_pairs={{0,8},{8,16},{16,24},{24,0},{1,9},{9,17},{17,25},{25,1},{2,10},{10... | collective-permute-start | bytes 1572872 | tf_op jit(solution)/shard_map/while/body/eval_jaxpr/ppermute | solution.py:12
  380.8 20.4 %collective-permute-start = (bf16[64,4096]{1,0:T(8,128)(2,1)}, bf16[64,4096]{1,0:T(8,128)(2,1)}, u32[]{:S(2)}, u32[]{:S(2)}) collective-permute-start(bf16[64,4096]{1,0:T(8,128)(2,1)} %copy.42), channel_id=1, source_target_pairs={{0,8},{8,16},{16,24},{24,0},{1,9},{9,17},{17,25},{25,1},{2,10},{10... | collective-permute-start | bytes 1572872 | tf_op jit(solution)/shard_map/while/body/eval_jaxpr/ppermute | solution.py:12
  403.7 16.0 %collective-permute-start.1 = (bf16[64,4096]{1,0:T(8,128)(2,1)}, bf16[64,4096]{1,0:T(8,128)(2,1)}, u32[]{:S(2)}, u32[]{:S(2)}) collective-permute-start(bf16[64,4096]{1,0:T(8,128)(2,1)} %fusion.64), channel_id=1, source_target_pairs={{0,8},{8,16},{16,24},{24,0},{1,9},{9,17},{17,25},{25,1},{2,10},{10... | collective-permute-start | bytes 1572872 | tf_op jit(solution)/shard_map/while/body/eval_jaxpr/ppermute | solution.py:12
  408.9 19.4 %collective-permute-start = (bf16[64,4096]{1,0:T(8,128)(2,1)}, bf16[64,4096]{1,0:T(8,128)(2,1)}, u32[]{:S(2)}, u32[]{:S(2)}) collective-permute-start(bf16[64,4096]{1,0:T(8,128)(2,1)} %copy.42), channel_id=1, source_target_pairs={{0,8},{8,16},{16,24},{24,0},{1,9},{9,17},{17,25},{25,1},{2,10},{10... | collective-permute-start | bytes 1572872 | tf_op jit(solution)/shard_map/while/body/eval_jaxpr/ppermute | solution.py:12
  430.7 16.1 %collective-permute-start.1 = (bf16[64,4096]{1,0:T(8,128)(2,1)}, bf16[64,4096]{1,0:T(8,128)(2,1)}, u32[]{:S(2)}, u32[]{:S(2)}) collective-permute-start(bf16[64,4096]{1,0:T(8,128)(2,1)} %fusion.64), channel_id=1, source_target_pairs={{0,8},{8,16},{16,24},{24,0},{1,9},{9,17},{17,25},{25,1},{2,10},{10... | collective-permute-start | bytes 1572872 | tf_op jit(solution)/shard_map/while/body/eval_jaxpr/ppermute | solution.py:12
  436.0 18.5 %collective-permute-start = (bf16[64,4096]{1,0:T(8,128)(2,1)}, bf16[64,4096]{1,0:T(8,128)(2,1)}, u32[]{:S(2)}, u32[]{:S(2)}) collective-permute-start(bf16[64,4096]{1,0:T(8,128)(2,1)} %copy.42), channel_id=1, source_target_pairs={{0,8},{8,16},{16,24},{24,0},{1,9},{9,17},{17,25},{25,1},{2,10},{10... | collective-permute-start | bytes 1572872 | tf_op jit(solution)/shard_map/while/body/eval_jaxpr/ppermute | solution.py:12
  456.2 5.8 copy-start.4
  462.0 1.5 copy-start
  462.0 1.5 copy-start.6
  566.7 40.9 %copy-start.2 = (bf16[256,4096]{1,0:T(8,128)(2,1)S(1)}, bf16[256,4096]{1,0:T(8,128)(2,1)}, u32[]{:S(2)}) copy-start(bf16[256,4096]{1,0:T(8,128)(2,1)} %param.11) | copy-start | bytes 6291460
  607.6 3.4 copy-start.1
Sparse Core Ops, SparseCore 0:
  53.7 36.2 all-gather.1
where the time goes:
time: 632 us; the launch traced here: 621 us
  waiting for transfers between devices  317 us (50%)
  local copies, waits for them, and re-layouts  125 us (20%)
  other arithmetic  97.1 us (15%)
  starting transfers between devices  33.3 us (5%)
  matrix products  33 us (5%)
  between operations  15.1 us (2%)
    all_to_all x1, waiting for transfers between devices, local(): lax.all_to_all(picked, 'grp', split_axis=0, concat_axis=0, tiled=True)  160 us
    all_to_all x1, waiting for transfers between devices, local(): lax.all_to_all(outgoing.reshape(groups, cap, width), 'grp', split_axis=0,...  81.5 us
    ppermute x8, waiting for transfers between devices, passed_along(): lax.ppermute(shard, axis, [(i, (i + by) % peers) for i in range(peers)])  62.7 us
    scatter-add x1, other arithmetic, local(): jax.ops.segment_sum(incoming.reshape(-1, width).astype(jnp.float32), requ...  40.9 us
    mul x5, local copies, waits for them, and re-layouts, local(): inv_temp * coef_hard.astype(jnp.float32)[:, :, None]  28.2 us
    scatter x1, other arithmetic, local(): jnp.zeros((groups * cap, width), jnp.bfloat16).at[place]  22.8 us
    gather x1, local copies, waits for them, and re-layouts, local(): reply.reshape(groups * cap, width)[place]  19.8 us
    reshape x2, local copies, waits for them, and re-layouts, local(): reply.reshape(groups * cap, width)[place]  17.7 us
  transfers between devices with their start and end apart: 12, of which 11 were waited for; matrix products, arithmetic and copies ran while one was open for 13% of the time, Pallas kernels for 0%

commit v1 on v0

v1 whole, which is shorter than its diff:
```python
import jax
import jax.numpy as jnp
from jax import lax
from jax.sharding import PartitionSpec as P

inv_temp = 50.0
eps = 1e-06


def unit_rows(rows):
    scale = lax.rsqrt(jnp.sum(rows * rows, axis=-1, keepdims=True) + eps)
    return (rows * scale, scale)


def unit_back(grad, unit, scale):
    return (grad - unit * jnp.sum(unit * grad, axis=-1, keepdims=True)) * scale


def cross(left, right):
    return lax.dot_general(
        left, right, (((1,), (1,)), ((), ())), preferred_element_type=jnp.float32
    )


def gather_back(coef, rows):
    return lax.dot_general(coef, rows, (((0,), (0,)), ((), ())), preferred_element_type=jnp.float32)


def local(queries, passages, pool, query_count, positive, neg_owner, neg_row):
    n_query, width = queries.shape
    n_pass = passages.shape[0]
    n_pool = pool.shape[0]
    groups = lax.axis_size("grp")
    loops = lax.axis_size("loop")
    me = lax.axis_index("grp")
    q_unit, q_scale = unit_rows(queries.astype(jnp.float32))
    p_unit, p_scale = unit_rows(passages.astype(jnp.float32))
    n_unit, n_scale = unit_rows(pool.astype(jnp.float32))
    q_hat = q_unit.astype(jnp.bfloat16)
    p_hat = p_unit.astype(jnp.bfloat16)
    n_hat = n_unit.astype(jnp.bfloat16)
    valid = lax.iota(jnp.int32, n_query) < query_count.reshape(())
    codes = jnp.where(valid[:, None], neg_owner * n_pool + neg_row, -1)
    valid = valid.astype(jnp.float32)[:, None]
    q_all = lax.all_gather(q_hat, "grp", axis=0, tiled=True)
    p_all = lax.all_gather(p_hat, "loop", axis=0, tiled=True)
    codes_all = lax.all_gather(codes, "grp", axis=0, tiled=True)

    scores = cross(q_hat, p_all) * inv_temp
    weights_in = jnp.exp(scores - inv_temp)
    total_in = jnp.sum(weights_in, axis=1)
    chosen = jnp.take_along_axis(scores, positive[:, None], axis=1)[:, 0]

    mine = me * n_pool + lax.iota(jnp.int32, n_pool)
    count = jnp.sum((codes_all[:, :, None] == mine[None, None, :]).astype(jnp.float32), axis=1)
    weights_hard = jnp.exp(cross(q_all, n_hat) * inv_temp - inv_temp)
    part = jnp.sum(weights_hard * count, axis=1)
    part = part + jnp.where(
        lax.iota(jnp.int32, groups)[:, None] == me, total_in[None, :], 0.0
    ).reshape(-1)
    total_all = lax.psum(part, "grp")
    total = lax.dynamic_slice_in_dim(total_all, me * n_query, n_query, 0)
    loss = valid[:, 0] * (jnp.log(total) + inv_temp - chosen)
    target = (positive[:, None] == lax.iota(jnp.int32, loops * n_pass)[None, :]).astype(jnp.float32)
    coef_in = (valid * (weights_in / total[:, None] - target)).astype(jnp.bfloat16)
    coef_hard = (count * (weights_hard / total_all[:, None])).astype(jnp.bfloat16)

    hard_part = jnp.dot(coef_hard, n_hat, preferred_element_type=jnp.float32).astype(jnp.bfloat16)
    hard_part = lax.psum_scatter(hard_part, "grp", scatter_dimension=0, tiled=True)
    pass_part = gather_back(coef_in, q_hat).astype(jnp.bfloat16)
    pass_part = lax.psum_scatter(pass_part, "loop", scatter_dimension=0, tiled=True)
    in_part = jnp.dot(coef_in, p_all, preferred_element_type=jnp.float32)
    pool_sum = gather_back(coef_hard, q_all)
    grad_query = unit_back(inv_temp * (in_part + hard_part.astype(jnp.float32)), q_unit, q_scale)
    grad_passage = unit_back(inv_temp * pass_part.astype(jnp.float32), p_unit, p_scale)
    grad_pool = unit_back(inv_temp * pool_sum, n_unit, n_scale)
    return (loss, grad_query, grad_passage, grad_pool)


def solution(mesh):
    return jax.shard_map(
        local,
        mesh=mesh,
        in_specs=(
            P(("loop", "grp"), None),
            P(("loop", "grp"), None),
            P(("loop", "grp"), None),
            P("loop", "grp"),
            P(("loop", "grp")),
            P(("loop", "grp"), None),
            P(("loop", "grp"), None),
        ),
        out_specs=(
            P(("loop", "grp")),
            P(("loop", "grp"), None),
            P(("loop", "grp"), None),
            P(("loop", "grp"), None),
        ),
        check_vma=False,
    )
```

time: 632 us -> 294 us (0.47); the launches traced: 621 us -> 290 us
  waiting for transfers between devices: 317 us -> 196 us
  local copies, waits for them, and re-layouts: 125 us -> 6.91 us
  other arithmetic: 97.1 us -> 18.4 us
  starting transfers between devices: 33.3 us -> 0.34 us
  blocking collectives: 0 us -> 27.4 us
  matrix products: 33 us -> 26.3 us
    all_to_all x3 -> x0, waiting for transfers between devices: 241 us -> none  [the longest x1 160 us: local(): lax.all_to_all(picked, 'grp', split_axis=0, concat_axis=0, tiled=True)]
    reduce_scatter x0 -> x2, waiting for transfers between devices: none -> 103 us  [the longest x1 85.5 us: local(): lax.psum_scatter(hard_part, 'grp', scatter_dimension=0, tiled=True)]
    all_gather x1 -> x2, waiting for transfers between devices: 13.1 us -> 92.2 us  [the longest x1 77.9 us: local(): q_all = lax.all_gather(q_hat, 'grp', axis=0, tiled=True)]
    ppermute x8 -> x0, waiting for transfers between devices: 62.7 us -> none  [passed_along(): lax.ppermute(shard, axis, [(i, (i + by) % peers) for i in range(peers)])]
    scatter-add x1 -> x0, other arithmetic: 40.9 us -> none  [local(): jax.ops.segment_sum(incoming.reshape(-1, width).astype(jnp.float32), requ...]
    gather x3 -> x0, local copies, waits for them, and re-layouts: 35.8 us -> none  [the longest x1 19.8 us: local(): reply.reshape(groups * cap, width)[place]]
    mul x7 -> x0, local copies, waits for them, and re-layouts: 28.5 us -> none  [the longest x5 28.2 us: local(): inv_temp * coef_hard.astype(jnp.float32)[:, :, None]]
    reshape x4 -> x0, local copies, waits for them, and re-layouts: 26.1 us -> none  [the longest x2 17.7 us: local(): reply.reshape(groups * cap, width)[place]]
  transfers between devices with their start and end apart: 12 -> 4, of which waited for: 11 -> 4; matrix products, arithmetic and copies ran while one was open for 13% -> 11% of each run, Pallas kernels for 0% -> 0%
where the time goes in v1:
time: 294 us; the launch traced here: 290 us
  waiting for transfers between devices  196 us (67%)
  blocking collectives  27.4 us (9%)
  matrix products  26.3 us (9%)
  other arithmetic  18.4 us (6%)
  between operations  14.7 us (5%)
  local copies, waits for them, and re-layouts  6.91 us (2%)
    reduce_scatter x1, waiting for transfers between devices, local(): lax.psum_scatter(hard_part, 'grp', scatter_dimension=0, tiled=True)  85.5 us
    all_gather x1, waiting for transfers between devices, local(): q_all = lax.all_gather(q_hat, 'grp', axis=0, tiled=True)  77.9 us
    reduce_scatter x1, waiting for transfers between devices, local(): lax.psum_scatter(pass_part, 'loop', scatter_dimension=0, tiled=True)  17.7 us
    all_gather x1, waiting for transfers between devices, local(): p_all = lax.all_gather(p_hat, 'loop', axis=0, tiled=True)  14.4 us
    all_gather x1, blocking collectives, local(): codes_all = lax.all_gather(codes, 'grp', axis=0, tiled=True)  14.2 us
    psum x1, blocking collectives, local(): total_all = lax.psum(part, 'grp')  13.2 us
    dot_general x2, matrix products, cross(): lax.dot_general(left, right, (((1,), (1,)), ((), ())), preferred_element_...  9.58 us
    dot_general x2, matrix products, gather_back(): lax.dot_general(coef, rows, (((0,), (0,)), ((), ())), preferred_element_t...  8.14 us
  transfers between devices with their start and end apart: 4, of which 4 were waited for; matrix products, arithmetic and copies ran while one was open for 11% of the time, Pallas kernels for 0%

profile of v1, /device:TPU:10, one launch (start us, length us, event | category | flops | bytes accessed | tf_op | source)
XLA Modules:
  0.0 289.5 jit_solution(17299324708866744297)
XLA Ops:
  7.2 1.3 fusion.23
  8.6 2.1 fusion.17
  11.0 1.2 fusion.10
  13.2 14.2 %all_gather.10 = s32[1024,7]{0,1:T(8,128)S(1)} all-gather(s32[128,7]{0,1:T(8,128)S(1)} %add_select_fusion), channel_id=1, replica_groups=mesh['loop'=4,'grp'=8] {'grp'}, dimensions={0}, use_global_device_ids=true | all-gather | bytes 32256 | tf_op jit(solution)/shard_map/all_gather | solution.py:47
  27.4 2.3 convert_reduce_fusion
  29.7 2.6 copy.13
  32.9 14.4 %all-gather.5.cloned.1.call-done = bf16[256,4096]{1,0:T(8,128)(2,1)} async-done(((bf16[64,4096]{1,0:T(8,128)(2,1)}), bf16[256,4096]{1,0:T(8,128)(2,1)}) %all-gather.5.cloned.1.call-update) | async-done | bytes 2097168 | tf_op jit(solution)/shard_map/all_gather | solution.py:46
  47.2 2.5 fusion.26
  49.7 1.5 gather_fusion
  51.2 77.9 %all-gather.3.cloned.1.call-done = bf16[1024,4096]{1,0:T(8,128)(2,1)} async-done(((bf16[128,4096]{1,0:T(8,128)(2,1)}), bf16[1024,4096]{1,0:T(8,128)(2,1)}) %all-gather.3.cloned.1.call-update) | async-done | bytes 8388624 | tf_op jit(solution)/shard_map/all_gather | solution.py:45
  129.1 7.1 %multiply_reduce_fusion = (f32[1024]{0:T(1024)S(1)}, f32[1024,256]{0,1:T(8,128)}) fusion(f32[1024,256]{0,1:T(8,128)} %copy.13, bf16[1024,4096]{1,0:T(8,128)(2,1)} %all-gather.3.cloned.1.call-done, bf16[256,4096]{1,0:T(8,128)(2,1)S(1)} %copy-done, f32[256]{0:T(256)S(1)} %add_rsqrt_fusion), kind=kOutput, calls=%fused_computation.40 | convolution fusion | flops 2151676928 | bytes 12588032 | tf_op jit(solution)/shard_map/dot_general | solution.py:20
  136.2 13.2 %psum.7 = f32[1024]{0:T(1024)S(1)} all-reduce(f32[1024]{0:T(1024)S(1)} %bitcast_add_fusion), channel_id=1, replica_groups=mesh['loop'=4,'grp'=8] {'grp'}, use_global_device_ids=true, to_apply=%region_6.7 | all-reduce | flops 1024 | bytes 8192 | tf_op jit(solution)/shard_map/psum | solution.py:61
  150.0 2.2 convolution_convert_fusion.1
  153.4 1.4 multiply_convert_fusion
  155.6 5.7 %convolution_convert_fusion = bf16[1024,4096]{1,0:T(8,128)(2,1)} fusion(bf16[1024,256]{0,1:T(8,128)(2,1)S(1)} %multiply_convert_fusion, bf16[256,4096]{1,0:T(8,128)(2,1)S(1)} %copy-done, f32[256]{0:T(256)S(1)} %add_rsqrt_fusion), kind=kOutput, calls=%fused_computation.1 | convolution fusion | flops 2154823680 | bytes 11011072 | tf_op jit(solution)/shard_map/dot_general | solution.py:68
  161.3 1.0 copy-done.7
  162.4 6.0 %fusion.4 = (f32[256]{0:T(256)S(1)}, f32[256,4096]{1,0:T(8,128)S(1)}) fusion(bf16[256,4096]{1,0:T(8,128)(2,1)S(1)} %copy-done, f32[256]{0:T(256)S(1)} %add_rsqrt_fusion, bf16[1024,256]{0,1:T(8,128)(2,1)S(1)} %copy-done.7, bf16[1024,4096]{1,0:T(8,128)(2,1)} %all-gather.3.cloned.1.call-done), kind=kOutput, calls=%fused_computation.12 | convolution fusion | flops 2152726272 | bytes 15206400 | tf_op jit(solution)/shard_map/dot_general | solution.py:26
  168.4 3.1 %fusion.6 = f32[256,4096]{1,0:T(8,128)} fusion(f32[256,4096]{1,0:T(8,128)S(1)} %get-tuple-element.13, bf16[256,4096]{1,0:T(8,128)(2,1)S(1)} %copy-done, f32[256]{0:T(256)S(1)} %get-tuple-element.12, f32[256]{0:T(256)S(1)} %add_rsqrt_fusion), kind=kLoop, calls=%fused_computation.14 | loop fusion | flops 5242880 | bytes 10487808 | tf_op jit(solution)/shard_map/mul | solution.py:16
  171.4 17.7 %reduce-scatter.5.cloned.1.call-done = bf16[64,4096]{1,0:T(8,128)(2,1)} async-done(((bf16[256,4096]{1,0:T(8,128)(2,1)}), bf16[64,4096]{1,0:T(8,128)(2,1)}) %reduce-scatter.5.cloned.1.call-update) | async-done | bytes 524304 | tf_op jit(solution)/shard_map/reduce_scatter | solution.py:71
  189.2 1.4 fusion.20
  190.6 2.3 fusion.22
  192.9 85.5 %reduce-scatter.3.cloned.1.call-done = bf16[128,4096]{1,0:T(8,128)(2,1)} async-done(((bf16[1024,4096]{1,0:T(8,128)(2,1)}), bf16[128,4096]{1,0:T(8,128)(2,1)}) %reduce-scatter.3.cloned.1.call-update) | async-done | bytes 1048592 | tf_op jit(solution)/shard_map/reduce_scatter | solution.py:69
  278.3 2.9 fusion.11
  281.2 1.8 fusion.13
  (45 shorter events, 3.7 us)
Async XLA Ops:
  7.2 3.5 %copy-start.2 = (bf16[128,4096]{1,0:T(8,128)(2,1)S(1)}, bf16[128,4096]{1,0:T(8,128)(2,1)}, u32[]{:S(2)}) copy-start(bf16[128,4096]{1,0:T(8,128)(2,1)} %param.7) | copy-start | bytes 3145732
  7.2 40.1 %all-gather.5.cloned.1.call-start = ((), (), s32[]{:S(2)}) async-start(), calls=%async_computation.3 | async-start | bytes 2621440 | tf_op jit(solution)/shard_map/all_gather | solution.py:46
  10.6 2.5 copy-start.9
  10.6 2.5 copy-start.10
  10.7 118.4 %all-gather.3.cloned.1.call-start = ((), (), s32[]{:S(2)}) async-start(), calls=%async_computation.2 | async-start | bytes 9437184 | tf_op jit(solution)/shard_map/all_gather | solution.py:45
  12.3 20.1 %copy-start.8 = (s32[128]{0:T(128)S(1)}, s32[128]{0:T(128)}, u32[]{:S(2)}) copy-start(s32[128]{0:T(128)} %param.11) | copy-start | bytes 1540
  12.3 20.1 %copy-start = (bf16[256,4096]{1,0:T(8,128)(2,1)S(1)}, bf16[256,4096]{1,0:T(8,128)(2,1)}, u32[]{:S(2)}) copy-start(bf16[256,4096]{1,0:T(8,128)(2,1)} %param.9) | copy-start | bytes 6291460
  12.3 176.9 %reduce-scatter.5.cloned.1.call-start = ((), (), s32[]{:S(2)}) async-start(), calls=%async_computation.5 | async-start | bytes 2621440 | tf_op jit(solution)/shard_map/reduce_scatter | solution.py:71
  29.7 17.6 %copy-start.1 = (bf16[128,4096]{1,0:T(8,128)(2,1)S(1)}, bf16[128,4096]{1,0:T(8,128)(2,1)}, u32[]{:S(2)}) copy-start(bf16[128,4096]{1,0:T(8,128)(2,1)} %fusion.10) | copy-start | bytes 3145732
  152.2 1.2 copy-start.5
  152.2 126.1 %reduce-scatter.3.cloned.1.call-start = ((), (), s32[]{:S(2)}) async-start(), calls=%async_computation.4 | async-start | bytes 9437184 | tf_op jit(solution)/shard_map/reduce_scatter | solution.py:69
  154.8 0.8 copy-start.6
  161.3 1.0 copy-start.7
  168.3 20.8 %copy-start.4 = (bf16[64,4096]{1,0:T(8,128)(2,1)S(1)}, bf16[64,4096]{1,0:T(8,128)(2,1)}, u32[]{:S(2)}) copy-start(bf16[64,4096]{1,0:T(8,128)(2,1)} %param.8) | copy-start | bytes 1572868
  171.4 106.9 %copy-start.3 = (bf16[128,4096]{1,0:T(8,128)(2,1)S(1)}, bf16[128,4096]{1,0:T(8,128)(2,1)}, u32[]{:S(2)}) copy-start(bf16[128,4096]{1,0:T(8,128)(2,1)} %param.7) | copy-start | bytes 3145732
Sparse Core Ops, SparseCore 0:
  10.8 36.4 all-gather.4
  49.4 79.6 all-gather.2
  152.3 36.8 reduce-scatter.4
  191.4 86.8 reduce-scatter.2

commit v2 on v1

v2 whole, which is shorter than its diff:
```python
import functools

import jax
import jax.numpy as jnp
from jax import lax
from jax.experimental import pallas as pl
from jax.experimental.pallas import tpu as pltpu
from jax.sharding import PartitionSpec as P

inv_temp = 50.0
eps = 1e-06
parts = 4
tile = 512


def unit_rows(rows):
    scale = lax.rsqrt(jnp.sum(rows * rows, axis=-1, keepdims=True) + eps)
    return (rows * scale, scale)


def unit_back(grad, unit, scale):
    return (grad - unit * jnp.sum(unit * grad, axis=-1, keepdims=True)) * scale


def cross(left, right):
    return lax.dot_general(
        left, right, (((1,), (1,)), ((), ())), preferred_element_type=jnp.float32
    )


def plain(left, right):
    return jnp.dot(left, right, preferred_element_type=jnp.float32)


def kernel(
    loops, chips,
    q_ref, p_ref, n_ref, code_ref, pos_ref, live_ref,
    loss_ref, dq_ref, dp_ref, dn_ref,
    q_all, n_sib, p_all, codes, weights, coef, totals,
    d_part, d_recv, dp_part, dp_recv, dn_part, dn_recv,
    ag_s, ag_r, rs_s, rs_r, tot_s, tot_r, code_s, code_r,
    p_s, p_r, dp_s, dp_r, sib_s, sib_r,
):
    loop = lax.axis_index("loop")
    me = lax.axis_index("grp")
    z = me // 2
    core = me % 2
    sib = z * 2 + 1 - core
    n_query, width = q_ref.shape
    n_pass = p_ref.shape[0]
    n_pool = n_ref.shape[0]
    rows = n_query // parts
    lanes = chips * rows
    passages = loops * n_pass
    tiles = width // tile

    def at_chip(chip):
        return (loop, chip * 2 + core)

    def peer_chip(off):
        return lax.rem(z + off, chips)

    def peer_loop(off):
        return lax.rem(loop + off, loops)

    def remote(src, dst, send, recv, device):
        return pltpu.make_async_remote_copy(
            src_ref=src, dst_ref=dst, send_sem=send, recv_sem=recv,
            device_id=device, device_id_type=pl.DeviceIdType.MESH,
        )

    barrier = pltpu.get_barrier_semaphore()
    for off in range(1, chips):
        pl.semaphore_signal(barrier, inc=1, device_id=at_chip(peer_chip(off)),
                            device_id_type=pl.DeviceIdType.MESH)
    for off in range(1, loops):
        pl.semaphore_signal(barrier, inc=1, device_id=(peer_loop(off), me),
                            device_id_type=pl.DeviceIdType.MESH)
    pl.semaphore_signal(barrier, inc=1, device_id=(loop, sib),
                        device_id_type=pl.DeviceIdType.MESH)
    pl.semaphore_wait(barrier, chips + loops - 1)

    def ag_copy(part, block, up, own=False):
        src = q_ref.at[pl.ds(part * rows, rows)] if own else q_all.at[part, block]
        way = 0 if up else 1
        chip = z + 1 if up else z - 1
        return remote(src, q_all.at[part, block], ag_s.at[part, block, way],
                      ag_r.at[part, block], at_chip(chip))

    def ag_own(part):
        @pl.when(z < chips - 1)
        def _():
            ag_copy(part, z, True, own=True).start()

        @pl.when(z > 0)
        def _():
            ag_copy(part, z, False, own=True).start()

    def ag_slot(part, step):
        @pl.when(z - step >= 0)
        def _():
            ag_copy(part, z - step, True).wait_recv()

            @pl.when(z < chips - 1)
            def _():
                ag_copy(part, z - step, True).start()

        @pl.when(z + step < chips)
        def _():
            ag_copy(part, z + step, False).wait_recv()

            @pl.when(z > 0)
            def _():
                ag_copy(part, z + step, False).start()

    def ag_drain(part):
        for step in range(chips):
            @pl.when((z - step >= 0) & (z < chips - 1))
            def _():
                ag_copy(part, z - step, True, own=step == 0).wait_send()

            @pl.when((z + step < chips) & (z > 0))
            def _():
                ag_copy(part, z + step, False, own=step == 0).wait_send()

    def rs_up(part, target):
        return remote(d_part.at[part, target], d_recv.at[part, target],
                      rs_s.at[part, target], rs_r.at[part, target], at_chip(z + 1))

    def rs_down(part, target):
        slot = jnp.where(target == z - 1, chips, target)
        return remote(d_part.at[part, target], d_recv.at[part, slot],
                      rs_s.at[part, target], rs_r.at[part, slot], at_chip(z - 1))

    def rs_arrived(part, slot):
        remote(d_part.at[part, 0], d_recv.at[part, slot],
               rs_s.at[part, 0], rs_r.at[part, slot], at_chip(z)).wait_recv()

    def rs_start(part):
        @pl.when(z == 0)
        def _():
            for target in range(chips - 1, 0, -1):
                rs_up(part, target).start()

        @pl.when(z == chips - 1)
        def _():
            for target in range(chips - 1):
                rs_down(part, target).start()

    def rs_add(part, target):
        d_part[part, target] = (
            d_part[part, target].astype(jnp.float32) + d_recv[part, target].astype(jnp.float32)
        ).astype(jnp.bfloat16)

    def rs_slot(part, step):
        @pl.when((z >= 1) & (step >= z))
        def _():
            target = chips - 1 - step + z
            rs_arrived(part, target)

            @pl.when(target > z)
            def _():
                rs_add(part, target)
                rs_up(part, target).start()

        @pl.when((z < chips - 1) & (step >= chips - 1 - z))
        def _():
            target = step - (chips - 1) + z
            rs_arrived(part, jnp.where(target == z, chips, target))

            @pl.when(target < z)
            def _():
                rs_add(part, target)
                rs_down(part, target).start()

    def rs_finish(part):
        mine = pl.ds(part * rows, rows)
        dq_ref[mine, :] = inv_temp * d_part[part, z].astype(jnp.float32)

        @pl.when(z > 0)
        def _():
            dq_ref[mine, :] += inv_temp * d_recv[part, z].astype(jnp.float32)

        @pl.when(z < chips - 1)
        def _():
            dq_ref[mine, :] += inv_temp * d_recv[part, chips].astype(jnp.float32)

    def rs_drain(part):
        for target in range(chips):
            @pl.when(z != target)
            def _():
                rs_up(part, target).wait_send()

    def tot_copy(part, off):
        return remote(totals.at[part, z], totals.at[part, z], tot_s.at[part, off],
                      tot_r.at[part, z], at_chip(peer_chip(off)))

    def code_copy(off):
        return remote(code_ref, codes.at[z], code_s.at[off], code_r.at[z],
                      at_chip(peer_chip(off)))

    def pass_copy(off):
        return remote(p_ref, p_all.at[loop], p_s.at[off], p_r.at[loop],
                      (peer_loop(off), me))

    def dp_copy(off):
        to = peer_loop(off)
        return remote(dp_part.at[to], dp_recv.at[loop], dp_s.at[off], dp_r.at[loop],
                      (to, me))

    pool_copy = remote(n_ref, n_sib, sib_s.at[0], sib_r.at[0], (loop, sib))
    dn_copy = remote(dn_part, dn_recv, sib_s.at[1], sib_r.at[1], (loop, sib))

    def q_cols(part, cols):
        return q_all[part, :, :, cols].reshape(lanes, tile)

    def p_cols(cols):
        return p_all[:, :, cols].reshape(passages, tile)

    def columns(i):
        return pl.ds(pl.multiple_of(i * tile, tile), tile)

    ag_own(0)
    for off in range(1, chips):
        code_copy(off).start()
    for off in range(1, loops):
        pass_copy(off).start()
    pool_copy.start()
    ag_own(1)
    for part in range(parts):
        q_all[part, z] = q_ref[pl.ds(part * rows, rows), :]
    p_all[loop] = p_ref[...]
    codes[z] = code_ref[...]
    for step in range(1, chips):
        ag_slot(0, step)
    for off in range(1, chips):
        chip = peer_chip(off)
        remote(code_ref, codes.at[chip], code_s.at[off], code_r.at[chip],
               at_chip(chip)).wait_recv()
    pool_copy.wait_recv()
    for off in range(1, loops):
        other = peer_loop(off)
        remote(p_ref, p_all.at[other], p_s.at[off], p_r.at[other], (other, me)).wait_recv()

    own_lane = lax.broadcasted_iota(jnp.int32, (1, lanes), 1) // rows == z
    top, bottom, end = n_pool, 2 * n_pool, 2 * n_pool + passages

    for part in range(parts):
        def add_scores(i, carry):
            cols = columns(i)
            q_tile = q_cols(part, cols)
            return (
                carry[0] + cross(n_ref[:, cols], q_tile),
                carry[1] + cross(n_sib[:, cols], q_tile),
                carry[2] + cross(p_cols(cols), q_tile),
            )

        s_own, s_sib, s_in = lax.fori_loop(
            0, tiles, add_scores,
            (jnp.zeros((n_pool, lanes), jnp.float32), jnp.zeros((n_pool, lanes), jnp.float32),
             jnp.zeros((passages, lanes), jnp.float32)),
        )
        part_codes = codes[0, part]
        for chip in range(1, chips):
            here = lax.broadcasted_iota(jnp.int32, part_codes.shape, 1) // rows == chip
            part_codes = jnp.where(here, codes[chip, part], part_codes)
        row_id = lax.broadcasted_iota(jnp.int32, (n_pool, lanes), 0)
        for first, owner, score in ((0, me, s_own), (top, sib, s_sib)):
            ids = row_id + owner * n_pool
            count = jnp.zeros((n_pool, lanes), jnp.float32)
            for k in range(part_codes.shape[0]):
                count += jnp.where(part_codes[k:k + 1, :] == ids, 1.0, 0.0)
            weights[0, first:first + n_pool, :] = count
            weights[1, first:first + n_pool, :] = jnp.exp(score * inv_temp - inv_temp)
        s_in = s_in * inv_temp
        weights[1, bottom:end, :] = jnp.exp(s_in - inv_temp)
        target = lax.broadcasted_iota(jnp.int32, (passages, lanes), 0) == pos_ref[part, 0:1, :]
        chosen = jnp.sum(jnp.where(target, s_in, 0.0), axis=0, keepdims=True)
        in_total = jnp.sum(weights[1, bottom:end, :], axis=0, keepdims=True)
        hard_total = jnp.sum(weights[0, 0:bottom, :] * weights[1, 0:bottom, :], axis=0,
                             keepdims=True)
        mine = hard_total + jnp.where(own_lane, in_total, 0.0)
        totals[part, z] = jnp.broadcast_to(mine, (8, lanes))
        for off in range(1, chips):
            tot_copy(part, off).start()

        if part + 2 < parts:
            ag_own(part + 2)
        for step in range(1, chips):
            if part + 1 < parts:
                ag_slot(part + 1, step)
            if part >= 1:
                rs_slot(part - 1, step)

        for off in range(1, chips):
            chip = peer_chip(off)
            remote(totals.at[part, z], totals.at[part, chip], tot_s.at[part, off],
                   tot_r.at[part, chip], at_chip(chip)).wait_recv()
        total = totals[part, 0, 0:1, :]
        for chip in range(1, chips):
            total = total + totals[part, chip, 0:1, :]
        live = live_ref[part, 0:1, :]
        loss_ref[part] = jnp.broadcast_to(
            jnp.where(own_lane, live * (jnp.log(total) + inv_temp - chosen), 0.0), (8, lanes)
        )
        share = weights[1, 0:bottom, :] / total
        share = share.astype(jnp.bfloat16).astype(jnp.float32) * weights[0, 0:bottom, :]
        inside = weights[1, bottom:end, :] / total - jnp.where(target, 1.0, 0.0)
        inside = jnp.where(own_lane, live * inside, 0.0)
        place = pl.ds(part * lanes, lanes)
        coef[0:bottom, place] = share.astype(jnp.bfloat16)
        coef[bottom:end, place] = inside.astype(jnp.bfloat16)
        back = jnp.transpose(share).astype(jnp.bfloat16)
        back_in = jnp.transpose(inside).astype(jnp.bfloat16)

        @pl.loop(0, tiles)
        def _(i):
            cols = columns(i)
            grad = plain(back[:, 0:top], n_ref[:, cols])
            grad += plain(back[:, top:bottom], n_sib[:, cols])
            grad += plain(back_in, p_cols(cols))
            d_part[part, :, :, cols] = grad.astype(jnp.bfloat16).reshape(chips, rows, tile)

        rs_start(part)

    def q_whole(cols):
        return q_all[:, :, :, cols].reshape(parts * lanes, tile)

    @pl.loop(0, tiles)
    def _(i):
        cols = columns(i)
        grad = plain(coef[bottom:end, :], q_whole(cols))
        dp_part[:, :, cols] = grad.astype(jnp.bfloat16).reshape(loops, n_pass, tile)

    for off in range(1, loops):
        dp_copy(off).start()
    rs_slot(parts - 1, 1)

    @pl.loop(0, tiles)
    def _(i):
        cols = columns(i)
        dn_part[:, cols] = plain(coef[top:bottom, :], q_whole(cols)).astype(jnp.bfloat16)

    dn_copy.start()
    for step in range(2, chips - 1):
        rs_slot(parts - 1, step)

    @pl.loop(0, tiles)
    def _(i):
        cols = columns(i)
        dn_ref[:, cols] = inv_temp * plain(coef[0:top, :], q_whole(cols))

    for part in range(parts - 1):
        rs_finish(part)
    dn_copy.wait_recv()

    @pl.loop(0, tiles)
    def _(i):
        cols = columns(i)
        dn_ref[:, cols] += inv_temp * dn_recv[:, cols].astype(jnp.float32)

    if chips > 2:
        rs_slot(parts - 1, chips - 1)
    dp_ref[...] = inv_temp * dp_part[loop].astype(jnp.float32)
    for off in range(1, loops):
        other = peer_loop(off)
        remote(dp_part.at[other], dp_recv.at[other], dp_s.at[off], dp_r.at[other],
               (other, me)).wait_recv()
        dp_ref[...] += inv_temp * dp_recv[other].astype(jnp.float32)
    rs_finish(parts - 1)

    for part in range(parts):
        ag_drain(part)
        rs_drain(part)
        for off in range(1, chips):
            tot_copy(part, off).wait_send()
    for off in range(1, chips):
        code_copy(off).wait_send()
    for off in range(1, loops):
        pass_copy(off).wait_send()
        dp_copy(off).wait_send()
    pool_copy.wait_send()
    dn_copy.wait_send()


def local(queries, passages, pool, query_count, positive, neg_owner, neg_row):
    n_query, width = queries.shape
    n_pass = passages.shape[0]
    n_pool = pool.shape[0]
    hard_count = neg_owner.shape[1]
    loops = lax.axis_size("loop")
    chips = lax.axis_size("grp") // 2
    rows = n_query // parts
    lanes = chips * rows
    q_unit, q_scale = unit_rows(queries.astype(jnp.float32))
    p_unit, p_scale = unit_rows(passages.astype(jnp.float32))
    n_unit, n_scale = unit_rows(pool.astype(jnp.float32))
    q_hat = q_unit.astype(jnp.bfloat16)
    p_hat = p_unit.astype(jnp.bfloat16)
    n_hat = n_unit.astype(jnp.bfloat16)
    valid = lax.iota(jnp.int32, n_query) < query_count.reshape(())

    def spread(flat):
        cut = jnp.transpose(flat.reshape(parts, rows, -1), (0, 2, 1))
        return jnp.tile(cut, (1, 1, chips))

    wanted = jnp.where(valid[:, None], neg_owner * n_pool + neg_row, -1)
    wanted = jnp.pad(wanted, ((0, 0), (0, -hard_count % 8)), constant_values=-1)
    wanted = spread(wanted)
    pos = jnp.broadcast_to(spread(positive[:, None]), (parts, 8, lanes))
    live = jnp.broadcast_to(spread(valid.astype(jnp.float32)[:, None]), (parts, 8, lanes))
    vmem = pl.BlockSpec(memory_space=pltpu.VMEM)
    dma = pltpu.SemaphoreType.DMA
    bf16, f32 = jnp.bfloat16, jnp.float32
    all_rows = 2 * n_pool + loops * n_pass
    loss, dq, dp, dn = pl.pallas_call(
        functools.partial(kernel, loops, chips),
        out_shape=(
            jax.ShapeDtypeStruct((parts, 8, lanes), f32),
            jax.ShapeDtypeStruct((n_query, width), f32),
            jax.ShapeDtypeStruct((n_pass, width), f32),
            jax.ShapeDtypeStruct((n_pool, width), f32),
        ),
        in_specs=[vmem] * 6,
        out_specs=(vmem,) * 4,
        scratch_shapes=[
            pltpu.VMEM((parts, chips, rows, width), bf16),
            pltpu.VMEM((n_pool, width), bf16),
            pltpu.VMEM((loops, n_pass, width), bf16),
            pltpu.VMEM((chips,) + wanted.shape, jnp.int32),
            pltpu.VMEM((2, all_rows, lanes), f32),
            pltpu.VMEM((all_rows, parts * lanes), bf16),
            pltpu.VMEM((parts, chips, 8, lanes), f32),
            pltpu.VMEM((parts, chips, rows, width), bf16),
            pltpu.VMEM((parts, chips + 1, rows, width), bf16),
            pltpu.VMEM((loops, n_pass, width), bf16),
            pltpu.VMEM((loops, n_pass, width), bf16),
            pltpu.VMEM((n_pool, width), bf16),
            pltpu.VMEM((n_pool, width), bf16),
            dma((parts, chips, 2)),
            dma((parts, chips)),
            dma((parts, chips)),
            dma((parts, chips + 1)),
            dma((parts, chips)),
            dma((parts, chips)),
            dma((chips,)),
            dma((chips,)),
            dma((loops,)),
            dma((loops,)),
            dma((loops,)),
            dma((loops,)),
            dma((2,)),
            dma((2,)),
        ],
        compiler_params=pltpu.CompilerParams(
            collective_id=0, has_side_effects=True, vmem_limit_bytes=62 * 1024 * 1024
        ),
    )(q_hat, p_hat, n_hat, wanted, pos, live)
    loss = jnp.sum(loss[:, 0, :].reshape(parts, chips, rows), axis=1).reshape(n_query)
    grad_query = unit_back(dq, q_unit, q_scale)
    grad_passage = unit_back(dp, p_unit, p_scale)
    grad_pool = unit_back(dn, n_unit, n_scale)
    return (loss, grad_query, grad_passage, grad_pool)


def solution(mesh):
    return jax.shard_map(
        local,
        mesh=mesh,
        in_specs=(
            P(("loop", "grp"), None),
            P(("loop", "grp"), None),
            P(("loop", "grp"), None),
            P("loop", "grp"),
            P(("loop", "grp")),
            P(("loop", "grp"), None),
            P(("loop", "grp"), None),
        ),
        out_specs=(
            P(("loop", "grp")),
            P(("loop", "grp"), None),
            P(("loop", "grp"), None),
            P(("loop", "grp"), None),
        ),
        check_vma=False,
    )
```

time: 294 us -> 175 us (0.60); the launches traced: 290 us -> 175 us
  waiting for transfers between devices: 196 us -> 0 us
  Pallas kernels: 0 us -> 151 us
  blocking collectives: 27.4 us -> 0 us
  matrix products: 26.3 us -> 0 us
  between operations: 14.7 us -> 1.51 us
    pallas_call x0 -> x1, Pallas kernels: none -> 151 us  [local(): pl.pallas_call(functools.partial(kernel, loops, chips), out_shape=(jax.Sh...]
    reduce_scatter x2 -> x0, waiting for transfers between devices: 103 us -> none  [the longest x1 85.5 us: local(): lax.psum_scatter(hard_part, 'grp', scatter_dimension=0, tiled=True)]
    all_gather x2 -> x0, waiting for transfers between devices: 92.2 us -> none  [the longest x1 77.9 us: local(): q_all = lax.all_gather(q_hat, 'grp', axis=0, tiled=True)]
    dot_general x6 -> x0, matrix products: 26.3 us -> none  [the longest x2 9.58 us: cross(): lax.dot_general(left, right, (((1,), (1,)), ((), ())), preferred_element_...]
    all_gather x1 -> x0, blocking collectives: 14.2 us -> none  [local(): codes_all = lax.all_gather(codes, 'grp', axis=0, tiled=True)]
    psum x1 -> x0, blocking collectives: 13.2 us -> none  [local(): total_all = lax.psum(part, 'grp')]
  transfers between devices with their start and end apart: 4 -> 0, of which waited for: 4 -> 0; matrix products, arithmetic and copies ran while one was open for 11% -> 0% of each run, Pallas kernels for 0% -> 0%
where the time goes in v2:
time: 175 us
  Pallas kernels  151 us (86%)
  other arithmetic  17 us (10%)
  local copies, waits for them, and re-layouts  4.92 us (3%)
    pallas_call x1, Pallas kernels, local(): pl.pallas_call(functools.partial(kernel, loops, chips), out_shape=(jax.Sh...  151 us
    mul x3, other arithmetic, unit_back(): return (grad - unit * jnp.sum(unit * grad, axis=-1, keepdims=True)) * scale  6.08 us

profile of v2, /device:TPU:10, one launch (start us, length us, event | category | flops | bytes accessed | tf_op | source)
XLA Modules:
  0.0 174.8 jit_solution(12319172599539503872)
XLA Ops:
  0.6 1.6 fusion.13
  2.2 2.6 %fusion.9.q_ref = bf16[128,4096]{1,0:T(8,128)(2,1)} fusion(bf16[128,4096]{1,0:T(8,128)(2,1)} %param.7, f32[128]{0:T(128)S(1)} %add_rsqrt_fusion.2), kind=kLoop, calls=%fused_computation.13 | loop fusion | flops 1572864 | bytes 2097664 | tf_op jit(solution)/shard_map/convert_element_type | solution.py:398
  4.8 0.2 fusion.20
  5.1 1.0 fusion.16.p_ref
  6.0 0.5 fusion.6
  6.6 1.9 %fusion.2.n_ref = bf16[256,4096]{1,0:T(8,128)(2,1)} fusion(bf16[256,4096]{1,0:T(8,128)(2,1)S(1)} %copy-done, f32[256]{0:T(256)S(1)} %add_rsqrt_fusion), kind=kLoop, calls=%fused_computation.4 | loop fusion | flops 3145728 | bytes 4195328 | tf_op jit(solution)/shard_map/convert_element_type | solution.py:400
  9.3 0.1 reshape.67
  9.4 0.7 tile.28.code_ref
  10.1 0.1 tile.29
  10.2 0.1 tile.31
  10.2 0.6 broadcast_in_dim.18.pos_ref
  10.9 0.1 tile.33
  11.0 0.6 broadcast_in_dim.19.live_ref
  11.6 151.3 %shard_map.102 = (f32[4,8,128]{2,1,0:T(8,128)}, f32[128,4096]{1,0:T(8,128)}, f32[64,4096]{1,0:T(8,128)}, f32[256,4096]{1,0:T(8,128)}) custom-call(bf16[128,4096]{1,0:T(8,128)(2,1)} %fusion.9.q_ref, bf16[64,4096]{1,0:T(8,128)(2,1)} %fusion.16.p_ref, bf16[256,4096]{1,0:T(8,128)(2,1)} %fusion.2.n_ref, s32[4,8,128]{2,1,0:T(8,128)} %tile.28.code_ref, ...), custom_call_target="tpu_custom_call" | custom-call | tf_op jit(solution)/shard_map/pallas_call | solution.py:416
  162.9 0.9 slice_reduce_fusion
  163.8 0.1 reshape_squeeze.3
  163.9 0.6 reshape.68
  164.5 2.1 %fusion.10 = f32[128]{0:T(128)S(1)} fusion(f32[128,4096]{1,0:T(8,128)} %get-tuple-element.9, bf16[128,4096]{1,0:T(8,128)(2,1)S(1)} %copy-done.3, f32[128]{0:T(128)S(1)} %add_rsqrt_fusion.2), kind=kLoop, calls=%fused_computation.14 | loop fusion | flops 2097024 | bytes 3146752 | tf_op jit(solution)/shard_map/reduce_sum | solution.py:22
  166.6 1.8 %fusion.12 = f32[128,4096]{1,0:T(8,128)} fusion(f32[128,4096]{1,0:T(8,128)S(1)} %copy-done.4, bf16[128,4096]{1,0:T(8,128)(2,1)S(1)} %copy-done.3, f32[128]{0:T(128)S(1)} %fusion.10, f32[128]{0:T(128)S(1)} %add_rsqrt_fusion.2), kind=kLoop, calls=%fused_computation.16 | loop fusion | flops 2621440 | bytes 5243904 | tf_op jit(solution)/shard_map/mul | solution.py:22
  168.4 0.3 fusion.17
  168.7 1.2 fusion.19
  170.0 1.0 copy-done.1
  171.0 0.7 fusion.3
  171.7 3.1 %fusion.5 = f32[256,4096]{1,0:T(8,128)} fusion(f32[256,4096]{1,0:T(8,128)S(1)} %copy-done.2, bf16[256,4096]{1,0:T(8,128)(2,1)S(1)} %copy-done.1, f32[256]{0:T(256)S(1)} %fusion.3, f32[256]{0:T(256)S(1)} %add_rsqrt_fusion), kind=kLoop, calls=%fused_computation.7 | loop fusion | flops 5242880 | bytes 10487808 | tf_op jit(solution)/shard_map/mul | solution.py:22
  (33 shorter events, 0.2 us)
Async XLA Ops:
  0.6 4.2 %copy-start.5 = (bf16[64,4096]{1,0:T(8,128)(2,1)S(1)}, bf16[64,4096]{1,0:T(8,128)(2,1)}, u32[]{:S(2)}) copy-start(bf16[64,4096]{1,0:T(8,128)(2,1)} %param.8) | copy-start | bytes 1572868
  2.2 3.8 %copy-start = (bf16[256,4096]{1,0:T(8,128)(2,1)S(1)}, bf16[256,4096]{1,0:T(8,128)(2,1)}, u32[]{:S(2)}) copy-start(bf16[256,4096]{1,0:T(8,128)(2,1)} %param.9) | copy-start | bytes 6291460
  6.5 2.7 %copy-start.8 = (s32[128,7]{0,1:T(8,128)S(1)}, s32[128,7]{0,1:T(8,128)}, u32[]{:S(2)}) copy-start(s32[128,7]{0,1:T(8,128)} %param.13) | copy-start | bytes 10756
  6.5 2.7 %copy-start.9 = (s32[128,7]{0,1:T(8,128)S(1)}, s32[128,7]{0,1:T(8,128)}, u32[]{:S(2)}) copy-start(s32[128,7]{0,1:T(8,128)} %param.12) | copy-start | bytes 10756
  6.5 3.5 %copy-start.10 = (s32[128]{0:T(128)S(1)}, s32[128]{0:T(128)}, u32[]{:S(2)}) copy-start(s32[128]{0:T(128)} %param.11) | copy-start | bytes 1540
  8.5 156.0 %copy-start.3 = (bf16[128,4096]{1,0:T(8,128)(2,1)S(1)}, bf16[128,4096]{1,0:T(8,128)(2,1)}, u32[]{:S(2)}) copy-start(bf16[128,4096]{1,0:T(8,128)(2,1)} %param.7) | copy-start | bytes 3145732
  162.9 3.7 %copy-start.4 = (f32[128,4096]{1,0:T(8,128)S(1)}, f32[128,4096]{1,0:T(8,128)}, u32[]{:S(2)}) copy-start(f32[128,4096]{1,0:T(8,128)} %get-tuple-element.9) | copy-start | bytes 6291460
  164.5 3.9 %copy-start.7 = (f32[64,4096]{1,0:T(8,128)S(1)}, f32[64,4096]{1,0:T(8,128)}, u32[]{:S(2)}) copy-start(f32[64,4096]{1,0:T(8,128)} %get-tuple-element.10) | copy-start | bytes 3145732
  166.6 1.8 %copy-start.6 = (bf16[64,4096]{1,0:T(8,128)(2,1)S(1)}, bf16[64,4096]{1,0:T(8,128)(2,1)}, u32[]{:S(2)}) copy-start(bf16[64,4096]{1,0:T(8,128)(2,1)} %param.8) | copy-start | bytes 1572868
  166.6 3.3 %copy-start.2 = (f32[256,4096]{1,0:T(8,128)S(1)}, f32[256,4096]{1,0:T(8,128)}, u32[]{:S(2)}) copy-start(f32[256,4096]{1,0:T(8,128)} %get-tuple-element.11) | copy-start | bytes 12582916
  168.4 2.6 %copy-start.1 = (bf16[256,4096]{1,0:T(8,128)(2,1)S(1)}, bf16[256,4096]{1,0:T(8,128)(2,1)}, u32[]{:S(2)}) copy-start(bf16[256,4096]{1,0:T(8,128)(2,1)} %param.9) | copy-start | bytes 6291460

commit v3 on v2

--- a/solution.py
+++ b/solution.py
@@ -11,14 +11,17 @@
 eps = 1e-06
 parts = 4
 tile = 512
-
-
-def unit_rows(rows):
-    scale = lax.rsqrt(jnp.sum(rows * rows, axis=-1, keepdims=True) + eps)
-    return (rows * scale, scale)
-
-
-def unit_back(grad, unit, scale):
+strip = 16
+
+
+def scale_of(rows):
+    return lax.rsqrt(jnp.sum(rows * rows, axis=-1, keepdims=True) + eps)
+
+
+def unit_back(grad, raw):
+    raw = raw.astype(jnp.float32)
+    scale = scale_of(raw)
+    unit = raw * scale
     return (grad - unit * jnp.sum(unit * grad, axis=-1, keepdims=True)) * scale
 
 
@@ -36,10 +39,10 @@
     loops, chips,
     q_ref, p_ref, n_ref, code_ref, pos_ref, live_ref,
     loss_ref, dq_ref, dp_ref, dn_ref,
-    q_all, n_sib, p_all, codes, weights, coef, totals,
-    d_part, d_recv, dp_part, dp_recv, dn_part, dn_recv,
+    q_all, n_own, n_sib, p_all, q_loop, codes, weights, coef, totals,
+    d_part, d_recv, c_part, c_recv, dn_part, dn_recv,
     ag_s, ag_r, rs_s, rs_r, tot_s, tot_r, code_s, code_r,
-    p_s, p_r, dp_s, dp_r, sib_s, sib_r,
+    p_s, p_r, ql_s, ql_r, c_s, c_r, sib_s, sib_r,
 ):
     loop = lax.axis_index("loop")
     me = lax.axis_index("grp")
@@ -78,23 +81,33 @@
                             device_id_type=pl.DeviceIdType.MESH)
     pl.semaphore_signal(barrier, inc=1, device_id=(loop, sib),
                         device_id_type=pl.DeviceIdType.MESH)
+
+    def unit_strip(raw):
+        raw = raw.astype(jnp.float32)
+        return (raw * scale_of(raw)).astype(jnp.bfloat16)
+
+    def unit_queries(part):
+        for low in range(0, rows, strip):
+            q_all[part, z, low:low + strip, :] = unit_strip(
+                q_ref[part * rows + low:part * rows + low + strip, :])
+
+    unit_queries(0)
     pl.semaphore_wait(barrier, chips + loops - 1)
 
-    def ag_copy(part, block, up, own=False):
-        src = q_ref.at[pl.ds(part * rows, rows)] if own else q_all.at[part, block]
+    def ag_copy(part, block, up):
         way = 0 if up else 1
         chip = z + 1 if up else z - 1
-        return remote(src, q_all.at[part, block], ag_s.at[part, block, way],
+        return remote(q_all.at[part, block], q_all.at[part, block], ag_s.at[part, block, way],
                       ag_r.at[part, block], at_chip(chip))
 
     def ag_own(part):
         @pl.when(z < chips - 1)
         def _():
-            ag_copy(part, z, True, own=True).start()
+            ag_copy(part, z, True).start()
 
         @pl.when(z > 0)
         def _():
-            ag_copy(part, z, False, own=True).start()
+            ag_copy(part, z, False).start()
 
     def ag_slot(part, step):
         @pl.when(z - step >= 0)
@@ -117,11 +130,11 @@
         for step in range(chips):
             @pl.when((z - step >= 0) & (z < chips - 1))
             def _():
-                ag_copy(part, z - step, True, own=step == 0).wait_send()
+                ag_copy(part, z - step, True).wait_send()
 
             @pl.when((z + step < chips) & (z > 0))
             def _():
-                ag_copy(part, z + step, False, own=step == 0).wait_send()
+                ag_copy(part, z + step, False).wait_send()
 
     def rs_up(part, target):
         return remote(d_part.at[part, target], d_recv.at[part, target],
@@ -174,16 +187,19 @@
                 rs_down(part, target).start()
 
     def rs_finish(part):
-        mine = pl.ds(part * rows, rows)
-        dq_ref[mine, :] = inv_temp * d_part[part, z].astype(jnp.float32)
+        dq_ref[pl.ds(part * rows, rows), :] = d_part[part, z].astype(jnp.float32)
 
         @pl.when(z > 0)
         def _():
-            dq_ref[mine, :] += inv_temp * d_recv[part, z].astype(jnp.float32)
+            dq_ref[pl.ds(part * rows, rows), :] += d_recv[part, z].astype(jnp.float32)
 
         @pl.when(z < chips - 1)
         def _():
-            dq_ref[mine, :] += inv_temp * d_recv[part, chips].astype(jnp.float32)
+            dq_ref[pl.ds(part * rows, rows), :] += d_recv[part, chips].astype(jnp.float32)
+
+        for low in range(part * rows, (part + 1) * rows, strip):
+            at = pl.ds(low, strip)
+            dq_ref[at, :] = unit_back(inv_temp * dq_ref[at, :], q_ref[at, :])
 
     def rs_drain(part):
         for target in range(chips):
@@ -200,15 +216,18 @@
                       at_chip(peer_chip(off)))
 
     def pass_copy(off):
-        return remote(p_ref, p_all.at[loop], p_s.at[off], p_r.at[loop],
+        return remote(p_all.at[loop], p_all.at[loop], p_s.at[off], p_r.at[loop],
                       (peer_loop(off), me))
 
-    def dp_copy(off):
+    def query_copy(part, off):
+        return remote(q_all.at[part, z], q_loop.at[loop, part], ql_s.at[part, off],
+                      ql_r.at[part, loop], (peer_loop(off), me))
+
+    def coef_copy(off):
         to = peer_loop(off)
-        return remote(dp_part.at[to], dp_recv.at[loop], dp_s.at[off], dp_r.at[loop],
-                      (to, me))
-
-    pool_copy = remote(n_ref, n_sib, sib_s.at[0], sib_r.at[0], (loop, sib))
+        return remote(c_part.at[to], c_recv.at[loop], c_s.at[off], c_r.at[loop], (to, me))
+
+    pool_copy = remote(n_own, n_sib, sib_s.at[0], sib_r.at[0], (loop, sib))
     dn_copy = remote(dn_part, dn_recv, sib_s.at[1], sib_r.at[1], (loop, sib))
 
     def q_cols(part, cols):
@@ -223,16 +242,31 @@
     ag_own(0)
     for off in range(1, chips):
         code_copy(off).start()
+
+    @pl.loop(0, n_pass // strip)
+    def _(i):
+        at = pl.ds(pl.multiple_of(i * strip, strip), strip)
+        p_all[loop, at, :] = unit_strip(p_ref[at, :])
+
     for off in range(1, loops):
         pass_copy(off).start()
+    unit_queries(1)
+    codes[z] = code_ref[...]
+    ag_slot(0, 1)
+    ag_own(1)
+
+    @pl.loop(0, n_pool // strip)
+    def _(i):
+        at = pl.ds(pl.multiple_of(i * strip, strip), strip)
+        n_own[at, :] = unit_strip(n_ref[at, :])
+
     pool_copy.start()
-    ag_own(1)
+    for part in range(2, parts):
+        unit_queries(part)
+    for step in range(2, chips):
+        ag_slot(0, step)
     for part in range(parts):
-        q_all[part, z] = q_ref[pl.ds(part * rows, rows), :]
-    p_all[loop] = p_ref[...]
-    codes[z] = code_ref[...]
-    for step in range(1, chips):
-        ag_slot(0, step)
+        q_loop[loop, part] = q_all[part, z]
     for off in range(1, chips):
         chip = peer_chip(off)
         remote(code_ref, codes.at[chip], code_s.at[off], code_r.at[chip],
@@ -240,17 +274,19 @@
     pool_copy.wait_recv()
     for off in range(1, loops):
         other = peer_loop(off)
-        remote(p_ref, p_all.at[other], p_s.at[off], p_r.at[other], (other, me)).wait_recv()
+        remote(p_all.at[other], p_all.at[other], p_s.at[off], p_r.at[other],
+               (other, me)).wait_recv()
 
     own_lane = lax.broadcasted_iota(jnp.int32, (1, lanes), 1) // rows == z
     top, bottom, end = n_pool, 2 * n_pool, 2 * n_pool + passages
+    c_sum = jnp.zeros((passages, n_query), jnp.float32)
 
     for part in range(parts):
         def add_scores(i, carry):
             cols = columns(i)
             q_tile = q_cols(part, cols)
             return (
-                carry[0] + cross(n_ref[:, cols], q_tile),
+                carry[0] + cross(n_own[:, cols], q_tile),
                 carry[1] + cross(n_sib[:, cols], q_tile),
                 carry[2] + cross(p_cols(cols), q_tile),
             )
@@ -284,13 +320,14 @@
         for off in range(1, chips):
             tot_copy(part, off).start()
 
-        if part + 2 < parts:
-            ag_own(part + 2)
-        for step in range(1, chips):
-            if part + 1 < parts:
-                ag_slot(part + 1, step)
-            if part >= 1:
-                rs_slot(part - 1, step)
+        for off in range(1, loops):
+            query_copy(part, off).start()
+        if part >= 1:
+            rs_slot(part - 1, 1)
+        if part + 1 < parts:
+            ag_slot(part + 1, 1)
+        if part >= 1 and chips > 2:
+            rs_slot(part - 1, 2)
 
         for off in range(1, chips):
             chip = peer_chip(off)
@@ -309,32 +346,37 @@
         inside = jnp.where(own_lane, live * inside, 0.0)
         place = pl.ds(part * lanes, lanes)
         coef[0:bottom, place] = share.astype(jnp.bfloat16)
-        coef[bottom:end, place] = inside.astype(jnp.bfloat16)
+        pick = lax.broadcasted_iota(jnp.int32, (lanes, n_query), 0) % rows + part * rows
+        pick = jnp.where(pick == lax.broadcasted_iota(jnp.int32, (lanes, n_query), 1), 1.0, 0.0)
+        c_sum = c_sum + plain(inside.astype(jnp.bfloat16), pick.astype(jnp.bfloat16))
         back = jnp.transpose(share).astype(jnp.bfloat16)
         back_in = jnp.transpose(inside).astype(jnp.bfloat16)
 
         @pl.loop(0, tiles)
         def _(i):
             cols = columns(i)
-            grad = plain(back[:, 0:top], n_ref[:, cols])
+            grad = plain(back[:, 0:top], n_own[:, cols])
             grad += plain(back[:, top:bottom], n_sib[:, cols])
             grad += plain(back_in, p_cols(cols))
             d_part[part, :, :, cols] = grad.astype(jnp.bfloat16).reshape(chips, rows, tile)
 
         rs_start(part)
+        if part + 2 < parts:
+            ag_own(part + 2)
+        if part >= 1:
+            for step in range(3, chips):
+                rs_slot(part - 1, step)
+        if part + 1 < parts:
+            for step in range(2, chips):
+                ag_slot(part + 1, step)
 
     def q_whole(cols):
         return q_all[:, :, :, cols].reshape(parts * lanes, tile)
 
-    @pl.loop(0, tiles)
-    def _(i):
-        cols = columns(i)
-        grad = plain(coef[bottom:end, :], q_whole(cols))
-        dp_part[:, :, cols] = grad.astype(jnp.bfloat16).reshape(loops, n_pass, tile)
-
+    c_part[...] = c_sum.astype(jnp.bfloat16).reshape(loops, n_pass, n_query)
+    c_recv[loop] = c_part[loop]
     for off in range(1, loops):
-        dp_copy(off).start()
-    rs_slot(parts - 1, 1)
+        coef_copy(off).start()
 
     @pl.loop(0, tiles)
     def _(i):
@@ -342,31 +384,48 @@
         dn_part[:, cols] = plain(coef[top:bottom, :], q_whole(cols)).astype(jnp.bfloat16)
 
     dn_copy.start()
-    for step in range(2, chips - 1):
-        rs_slot(parts - 1, step)
+    rs_slot(parts - 1, 1)
 
     @pl.loop(0, tiles)
     def _(i):
         cols = columns(i)
-        dn_ref[:, cols] = inv_temp * plain(coef[0:top, :], q_whole(cols))
-
+        dn_ref[:, cols] = plain(coef[0:top, :], q_whole(cols))
+
+    if chips > 2:
+        rs_slot(parts - 1, 2)
     for part in range(parts - 1):
         rs_finish(part)
-    dn_copy.wait_recv()
-
-    @pl.loop(0, tiles)
-    def _(i):
-        cols = columns(i)
-        dn_ref[:, cols] += inv_temp * dn_recv[:, cols].astype(jnp.float32)
-
-    if chips > 2:
-        rs_slot(parts - 1, chips - 1)
-    dp_ref[...] = inv_temp * dp_part[loop].astype(jnp.float32)
     for off in range(1, loops):
         other = peer_loop(off)
-        remote(dp_part.at[other], dp_recv.at[other], dp_s.at[off], dp_r.at[other],
+        remote(c_part.at[other], c_recv.at[other], c_s.at[off], c_r.at[other],
                (other, me)).wait_recv()
-        dp_ref[...] += inv_temp * dp_recv[other].astype(jnp.float32)
+        for part in range(parts):
+            remote(q_all.at[part, z], q_loop.at[other, part], ql_s.at[part, off],
+                   ql_r.at[part, other], (other, me)).wait_recv()
+
+    @pl.loop(0, tiles)
+    def _(i):
+        cols = columns(i)
+        grad = jnp.zeros((n_pass, tile), jnp.float32)
+        for other in range(loops):
+            grad += plain(c_recv[other], q_loop[other, :, :, cols].reshape(n_query, tile))
+        dp_ref[:, cols] = inv_temp * grad
+
+    @pl.loop(0, n_pass // strip)
+    def _(i):
+        at = pl.ds(pl.multiple_of(i * strip, strip), strip)
+        dp_ref[at, :] = unit_back(dp_ref[at, :], p_ref[at, :])
+
+    dn_copy.wait_recv()
+
+    @pl.loop(0, n_pool // strip)
+    def _(i):
+        at = pl.ds(pl.multiple_of(i * strip, strip), strip)
+        grad = inv_temp * (dn_ref[at, :] + dn_recv[at, :].astype(jnp.float32))
+        dn_ref[at, :] = unit_back(grad, n_ref[at, :])
+
+    for step in range(3, chips):
+        rs_slot(parts - 1, step)
     rs_finish(parts - 1)
 
     for part in range(parts):
@@ -378,7 +437,9 @@
         code_copy(off).wait_send()
     for off in range(1, loops):
         pass_copy(off).wait_send()
-        dp_copy(off).wait_send()
+        coef_copy(off).wait_send()
+        for part in range(parts):
+            query_copy(part, off).wait_send()
     pool_copy.wait_send()
     dn_copy.wait_send()
 
@@ -392,12 +453,6 @@
     chips = lax.axis_size("grp") // 2
     rows = n_query // parts
     lanes = chips * rows
-    q_unit, q_scale = unit_rows(queries.astype(jnp.float32))
-    p_unit, p_scale = unit_rows(passages.astype(jnp.float32))
-    n_unit, n_scale = unit_rows(pool.astype(jnp.float32))
-    q_hat = q_unit.astype(jnp.bfloat16)
-    p_hat = p_unit.astype(jnp.bfloat16)
-    n_hat = n_unit.astype(jnp.bfloat16)
     valid = lax.iota(jnp.int32, n_query) < query_count.reshape(())
 
     def spread(flat):
@@ -413,7 +468,7 @@
     dma = pltpu.SemaphoreType.DMA
     bf16, f32 = jnp.bfloat16, jnp.float32
     all_rows = 2 * n_pool + loops * n_pass
-    loss, dq, dp, dn = pl.pallas_call(
+    loss, grad_query, grad_passage, grad_pool = pl.pallas_call(
         functools.partial(kernel, loops, chips),
         out_shape=(
             jax.ShapeDtypeStruct((parts, 8, lanes), f32),
@@ -426,15 +481,17 @@
         scratch_shapes=[
             pltpu.VMEM((parts, chips, rows, width), bf16),
             pltpu.VMEM((n_pool, width), bf16),
+            pltpu.VMEM((n_pool, width), bf16),
             pltpu.VMEM((loops, n_pass, width), bf16),
+            pltpu.VMEM((loops, parts, rows, width), bf16),
             pltpu.VMEM((chips,) + wanted.shape, jnp.int32),
             pltpu.VMEM((2, all_rows, lanes), f32),
-            pltpu.VMEM((all_rows, parts * lanes), bf16),
+            pltpu.VMEM((2 * n_pool, parts * lanes), bf16),
             pltpu.VMEM((parts, chips, 8, lanes), f32),
             pltpu.VMEM((parts, chips, rows, width), bf16),
             pltpu.VMEM((parts, chips + 1, rows, width), bf16),
-            pltpu.VMEM((loops, n_pass, width), bf16),
-            pltpu.VMEM((loops, n_pass, width), bf16),
+            pltpu.VMEM((loops, n_pass, n_query), bf16),
+            pltpu.VMEM((loops, n_pass, n_query), bf16),
             pltpu.VMEM((n_pool, width), bf16),
             pltpu.VMEM((n_pool, width), bf16),
             dma((parts, chips, 2)),
@@ -447,19 +504,18 @@
             dma((chips,)),
             dma((loops,)),
             dma((loops,)),
+            dma((parts, loops)),
+            dma((parts, loops)),
             dma((loops,)),
             dma((loops,)),
             dma((2,)),
             dma((2,)),
         ],
         compiler_params=pltpu.CompilerParams(
-            collective_id=0, has_side_effects=True, vmem_limit_bytes=62 * 1024 * 1024
+            collective_id=0, has_side_effects=True, vmem_limit_bytes=63 * 1024 * 1024
         ),
-    )(q_hat, p_hat, n_hat, wanted, pos, live)
+    )(queries, passages, pool, wanted, pos, live)
     loss = jnp.sum(loss[:, 0, :].reshape(parts, chips, rows), axis=1).reshape(n_query)
-    grad_query = unit_back(dq, q_unit, q_scale)
-    grad_passage = unit_back(dp, p_unit, p_scale)
-    grad_pool = unit_back(dn, n_unit, n_scale)
     return (loss, grad_query, grad_passage, grad_pool)
 
 

time: 175 us -> 155 us (0.89); the launches traced: 175 us -> 153 us
  other arithmetic: 17 us -> 0.74 us
  Pallas kernels: 151 us -> 139 us
  local copies, waits for them, and re-layouts: 4.92 us -> 11.9 us
    pallas_call x1, Pallas kernels: 151 us -> 139 us  [local(): pl.pallas_call(functools.partial(kernel, loops, chips), out_shape=(jax.Sh...]
    unnamed x22 -> x5, local copies, waits for them, and re-layouts: 1.08 us -> 7.55 us
    mul x3 -> x0, other arithmetic: 6.08 us -> none  [unit_back(): return (grad - unit * jnp.sum(unit * grad, axis=-1, keepdims=True)) * scale]
    convert_element_type x3 -> x0, other arithmetic: 5.47 us -> none  [the longest x1 2.6 us: local(): q_hat = q_unit.astype(jnp.bfloat16)]
    reduce_sum x6 -> x0, other arithmetic: 5.41 us -> none  [the longest x3 3.13 us: unit_back(): return (grad - unit * jnp.sum(unit * grad, axis=-1, keepdims=True)) * scale]
where the time goes in v3:
time: 155 us; the launch traced here: 153 us
  Pallas kernels  139 us (90%)
  local copies, waits for them, and re-layouts  11.9 us (8%)
    pallas_call x1, Pallas kernels, local(): pl.pallas_call(functools.partial(kernel, loops, chips), out_shape=(jax.Sh...  139 us
    unnamed x5, local copies, waits for them, and re-layouts  7.55 us

profile of v3, /device:TPU:10, one launch (start us, length us, event | category | flops | bytes accessed | tf_op | source)
XLA Modules:
  0.0 152.7 jit_solution(17711731010687124060)
XLA Ops:
  1.3 0.7 tile.29
  2.0 0.7 add_select_fusion
  2.8 0.1 tile.33
  2.8 0.1 tile.31
  2.9 0.1 reshape.46
  3.0 0.6 broadcast_in_dim.25.pos_ref
  3.6 0.6 broadcast_in_dim.26.live_ref
  4.2 0.7 tile.28.code_ref
  4.9 138.8 %shard_map.102 = (f32[4,8,128]{2,1,0:T(8,128)}, f32[128,4096]{1,0:T(8,128)}, f32[64,4096]{1,0:T(8,128)}, f32[256,4096]{1,0:T(8,128)}) custom-call(bf16[128,4096]{1,0:T(8,128)(2,1)} %q_ref.1, bf16[64,4096]{1,0:T(8,128)(2,1)} %p_ref.1, bf16[256,4096]{1,0:T(8,128)(2,1)} %n_ref.1, s32[4,8,128]{2,1,0:T(8,128)} %tile.28.code_ref, ...), custom_call_target="tpu_custom_call" | custom-call | tf_op jit(solution)/shard_map/pallas_call | solution.py:471
  143.7 0.7 slice_reduce_fusion
  144.5 0.1 reshape_squeeze.3
  144.6 0.6 reshape.47
  145.2 0.0 copy-start
  145.2 3.3 %copy.16 = f32[128,4096]{1,0:T(8,128)} copy(f32[128,4096]{1,0:T(8,128)} %get-tuple-element.17) | data formatting | bytes 4194304
  148.4 2.3 %copy.17 = f32[64,4096]{1,0:T(8,128)} copy(f32[64,4096]{1,0:T(8,128)} %get-tuple-element.18) | data formatting | bytes 2097152
  150.7 0.0 copy-done
  150.7 2.0 %copy.18 = f32[256,4096]{1,0:T(8,128)} copy(f32[256,4096]{1,0:T(8,128)S(1)} %copy-done) | data formatting | bytes 8388608
  (8 shorter events, 0.1 us)
Async XLA Ops:
  145.2 5.5 %copy-start = (f32[256,4096]{1,0:T(8,128)S(1)}, f32[256,4096]{1,0:T(8,128)}, u32[]{:S(2)}) copy-start(f32[256,4096]{1,0:T(8,128)} %get-tuple-element.19) | copy-start | bytes 12582916

commit v4 on v3

--- a/solution.py
+++ b/solution.py
@@ -9,7 +9,8 @@
 
 inv_temp = 50.0
 eps = 1e-06
-parts = 4
+parts = 8
+ahead = 2
 tile = 512
 strip = 16
 
@@ -36,8 +37,8 @@
 
 
 def kernel(
-    loops, chips,
-    q_ref, p_ref, n_ref, code_ref, pos_ref, live_ref,
+    loops, chips, hard_count,
+    q_ref, p_ref, n_ref, code_ref,
     loss_ref, dq_ref, dp_ref, dn_ref,
     q_all, n_own, n_sib, p_all, q_loop, codes, weights, coef, totals,
     d_part, d_recv, c_part, c_recv, dn_part, dn_recv,
@@ -101,11 +102,17 @@
                       ag_r.at[part, block], at_chip(chip))
 
     def ag_own(part):
-        @pl.when(z < chips - 1)
+        @pl.when((z < chips - 1) & (z > 0))
         def _():
             ag_copy(part, z, True).start()
-
-        @pl.when(z > 0)
+            ag_copy(part, z, False).start()
+
+    def ag_ends(part):
+        @pl.when(z == 0)
+        def _():
+            ag_copy(part, z, True).start()
+
+        @pl.when(z == chips - 1)
         def _():
             ag_copy(part, z, False).start()
 
@@ -240,6 +247,7 @@
         return pl.ds(pl.multiple_of(i * tile, tile), tile)
 
     ag_own(0)
+    ag_ends(0)
     for off in range(1, chips):
         code_copy(off).start()
 
@@ -252,8 +260,14 @@
         pass_copy(off).start()
     unit_queries(1)
     codes[z] = code_ref[...]
+    ag_ends(1)
     ag_slot(0, 1)
     ag_own(1)
+    for part in range(2, parts):
+        unit_queries(part)
+        ag_ends(part)
+    for step in range(2, chips):
+        ag_slot(0, step)
 
     @pl.loop(0, n_pool // strip)
     def _(i):
@@ -261,10 +275,11 @@
         n_own[at, :] = unit_strip(n_ref[at, :])
 
     pool_copy.start()
-    for part in range(2, parts):
-        unit_queries(part)
-    for step in range(2, chips):
-        ag_slot(0, step)
+    for part in range(1, ahead):
+        ag_slot(part, 1)
+        ag_own(part + 1)
+        for step in range(2, chips):
+            ag_slot(part, step)
     for part in range(parts):
         q_loop[loop, part] = q_all[part, z]
     for off in range(1, chips):
@@ -304,13 +319,14 @@
         for first, owner, score in ((0, me, s_own), (top, sib, s_sib)):
             ids = row_id + owner * n_pool
             count = jnp.zeros((n_pool, lanes), jnp.float32)
-            for k in range(part_codes.shape[0]):
+            for k in range(hard_count):
                 count += jnp.where(part_codes[k:k + 1, :] == ids, 1.0, 0.0)
             weights[0, first:first + n_pool, :] = count
             weights[1, first:first + n_pool, :] = jnp.exp(score * inv_temp - inv_temp)
         s_in = s_in * inv_temp
+        positive = code_ref[part, hard_count:hard_count + 1, :]
         weights[1, bottom:end, :] = jnp.exp(s_in - inv_temp)
-        target = lax.broadcasted_iota(jnp.int32, (passages, lanes), 0) == pos_ref[part, 0:1, :]
+        target = lax.broadcasted_iota(jnp.int32, (passages, lanes), 0) == positive
         chosen = jnp.sum(jnp.where(target, s_in, 0.0), axis=0, keepdims=True)
         in_total = jnp.sum(weights[1, bottom:end, :], axis=0, keepdims=True)
         hard_total = jnp.sum(weights[0, 0:bottom, :] * weights[1, 0:bottom, :], axis=0,
@@ -324,8 +340,8 @@
             query_copy(part, off).start()
         if part >= 1:
             rs_slot(part - 1, 1)
-        if part + 1 < parts:
-            ag_slot(part + 1, 1)
+        if part + ahead < parts:
+            ag_slot(part + ahead, 1)
         if part >= 1 and chips > 2:
             rs_slot(part - 1, 2)
 
@@ -336,7 +352,7 @@
         total = totals[part, 0, 0:1, :]
         for chip in range(1, chips):
             total = total + totals[part, chip, 0:1, :]
-        live = live_ref[part, 0:1, :]
+        live = jnp.where(positive >= 0, 1.0, 0.0)
         loss_ref[part] = jnp.broadcast_to(
             jnp.where(own_lane, live * (jnp.log(total) + inv_temp - chosen), 0.0), (8, lanes)
         )
@@ -361,14 +377,14 @@
             d_part[part, :, :, cols] = grad.astype(jnp.bfloat16).reshape(chips, rows, tile)
 
         rs_start(part)
-        if part + 2 < parts:
-            ag_own(part + 2)
+        if part + ahead + 1 < parts:
+            ag_own(part + ahead + 1)
         if part >= 1:
             for step in range(3, chips):
                 rs_slot(part - 1, step)
-        if part + 1 < parts:
+        if part + ahead < parts:
             for step in range(2, chips):
-                ag_slot(part + 1, step)
+                ag_slot(part + ahead, step)
 
     def q_whole(cols):
         return q_all[:, :, :, cols].reshape(parts * lanes, tile)
@@ -455,28 +471,24 @@
     lanes = chips * rows
     valid = lax.iota(jnp.int32, n_query) < query_count.reshape(())
 
-    def spread(flat):
-        cut = jnp.transpose(flat.reshape(parts, rows, -1), (0, 2, 1))
-        return jnp.tile(cut, (1, 1, chips))
-
-    wanted = jnp.where(valid[:, None], neg_owner * n_pool + neg_row, -1)
-    wanted = jnp.pad(wanted, ((0, 0), (0, -hard_count % 8)), constant_values=-1)
-    wanted = spread(wanted)
-    pos = jnp.broadcast_to(spread(positive[:, None]), (parts, 8, lanes))
-    live = jnp.broadcast_to(spread(valid.astype(jnp.float32)[:, None]), (parts, 8, lanes))
+    wanted = jnp.concatenate([neg_owner * n_pool + neg_row, positive[:, None]], axis=1)
+    wanted = jnp.where(valid[:, None], wanted, -1)
+    wanted = jnp.pad(wanted, ((0, 0), (0, -(hard_count + 1) % 8)), constant_values=-1)
+    wanted = jnp.transpose(wanted.reshape(parts, rows, -1), (0, 2, 1))
+    wanted = jnp.tile(wanted, (1, 1, chips))
     vmem = pl.BlockSpec(memory_space=pltpu.VMEM)
     dma = pltpu.SemaphoreType.DMA
     bf16, f32 = jnp.bfloat16, jnp.float32
     all_rows = 2 * n_pool + loops * n_pass
     loss, grad_query, grad_passage, grad_pool = pl.pallas_call(
-        functools.partial(kernel, loops, chips),
+        functools.partial(kernel, loops, chips, hard_count),
         out_shape=(
             jax.ShapeDtypeStruct((parts, 8, lanes), f32),
             jax.ShapeDtypeStruct((n_query, width), f32),
             jax.ShapeDtypeStruct((n_pass, width), f32),
             jax.ShapeDtypeStruct((n_pool, width), f32),
         ),
-        in_specs=[vmem] * 6,
+        in_specs=[vmem] * 4,
         out_specs=(vmem,) * 4,
         scratch_shapes=[
             pltpu.VMEM((parts, chips, rows, width), bf16),
@@ -514,7 +526,7 @@
         compiler_params=pltpu.CompilerParams(
             collective_id=0, has_side_effects=True, vmem_limit_bytes=63 * 1024 * 1024
         ),
-    )(queries, passages, pool, wanted, pos, live)
+    )(queries, passages, pool, wanted)
     loss = jnp.sum(loss[:, 0, :].reshape(parts, chips, rows), axis=1).reshape(n_query)
     return (loss, grad_query, grad_passage, grad_pool)
 

time: 155 us -> 177 us (1.14); the launches traced: 153 us -> 177 us
  Pallas kernels: 139 us -> 165 us
  local copies, waits for them, and re-layouts: 11.9 us -> 9.27 us
    pallas_call x1, Pallas kernels: 139 us -> 165 us  [local(): pl.pallas_call(functools.partial(kernel, loops, chips, hard_count), out_s...]
    unnamed x5 -> x7, local copies, waits for them, and re-layouts: 7.55 us -> 6.25 us
where the time goes in v4:
time: 177 us
  Pallas kernels  165 us (93%)
  local copies, waits for them, and re-layouts  9.27 us (5%)
    pallas_call x1, Pallas kernels, local(): pl.pallas_call(functools.partial(kernel, loops, chips, hard_count), out_s...  165 us
    unnamed x7, local copies, waits for them, and re-layouts  6.25 us

profile of v4, /device:TPU:10, one launch (start us, length us, event | category | flops | bytes accessed | tf_op | source)
XLA Modules:
  0.0 176.7 jit_solution(7488030379769583104)
XLA Ops:
  1.3 0.7 concatenate.9
  2.0 0.7 multiply_add_fusion
  2.7 0.1 concatenate.8
  2.9 0.7 tile.10.code_ref
  3.6 165.3 %shard_map.102 = (f32[8,8,64]{2,1,0:T(8,128)}, f32[128,4096]{1,0:T(8,128)}, f32[64,4096]{1,0:T(8,128)}, f32[256,4096]{1,0:T(8,128)}) custom-call(bf16[128,4096]{1,0:T(8,128)(2,1)} %q_ref.1, bf16[64,4096]{1,0:T(8,128)(2,1)} %p_ref.1, bf16[256,4096]{1,0:T(8,128)(2,1)} %n_ref.1, s32[8,8,64]{2,1,0:T(8,128)} %tile.10.code_ref), custom_call_target="tpu_custom_call" | custom-call | tf_op jit(solution)/shard_map/pallas_call | solution.py:483
  168.9 0.8 slice_reduce_fusion
  169.7 0.0 copy-start.1
  169.7 0.1 reshape_squeeze.3
  169.8 0.6 reshape.32
  170.4 0.0 copy-start
  170.4 3.3 %copy.16 = f32[128,4096]{1,0:T(8,128)} copy(f32[128,4096]{1,0:T(8,128)} %get-tuple-element.17) | data formatting | bytes 4194304
  173.7 0.0 copy-done.1
  173.7 1.0 copy.17
  174.7 0.0 copy-done
  174.7 2.0 %copy.18 = f32[256,4096]{1,0:T(8,128)} copy(f32[256,4096]{1,0:T(8,128)S(1)} %copy-done) | data formatting | bytes 8388608
  (5 shorter events, 0.1 us)
Async XLA Ops:
  169.7 4.0 %copy-start.1 = (f32[64,4096]{1,0:T(8,128)S(1)}, f32[64,4096]{1,0:T(8,128)}, u32[]{:S(2)}) copy-start(f32[64,4096]{1,0:T(8,128)} %get-tuple-element.18) | copy-start | bytes 3145732
  170.4 4.2 %copy-start = (f32[256,4096]{1,0:T(8,128)S(1)}, f32[256,4096]{1,0:T(8,128)}, u32[]{:S(2)}) copy-start(f32[256,4096]{1,0:T(8,128)} %get-tuple-element.19) | copy-start | bytes 12582916

commit v5 on v4

--- a/solution.py
+++ b/solution.py
@@ -9,9 +9,9 @@
 
 inv_temp = 50.0
 eps = 1e-06
-parts = 8
-ahead = 2
-tile = 512
+parts = 4
+ahead = 1
+tile = 1024
 strip = 16
 
 

time: 177 us -> 148 us (0.84)
  Pallas kernels: 165 us -> 135 us
    pallas_call x1, Pallas kernels: 165 us -> 135 us  [local(): pl.pallas_call(functools.partial(kernel, loops, chips, hard_count), out_s...]
    unnamed x7 -> x5, local copies, waits for them, and re-layouts: 6.25 us -> 7.55 us
where the time goes in v5:
time: 148 us
  Pallas kernels  135 us (91%)
  local copies, waits for them, and re-layouts  10.5 us (7%)
    pallas_call x1, Pallas kernels, local(): pl.pallas_call(functools.partial(kernel, loops, chips, hard_count), out_s...  135 us
    unnamed x5, local copies, waits for them, and re-layouts  7.55 us

profile of v5, /device:TPU:10, one launch (start us, length us, event | category | flops | bytes accessed | tf_op | source)
XLA Modules:
  0.0 147.5 jit_solution(6227684599330733801)
XLA Ops:
  1.3 0.7 concatenate.9
  2.0 0.7 multiply_add_fusion
  2.7 0.1 concatenate.8
  2.9 0.7 tile.10.code_ref
  3.6 135.0 %shard_map.102 = (f32[4,8,128]{2,1,0:T(8,128)}, f32[128,4096]{1,0:T(8,128)}, f32[64,4096]{1,0:T(8,128)}, f32[256,4096]{1,0:T(8,128)}) custom-call(bf16[128,4096]{1,0:T(8,128)(2,1)} %q_ref.1, bf16[64,4096]{1,0:T(8,128)(2,1)} %p_ref.1, bf16[256,4096]{1,0:T(8,128)(2,1)} %n_ref.1, s32[4,8,128]{2,1,0:T(8,128)} %tile.10.code_ref), custom_call_target="tpu_custom_call" | custom-call | tf_op jit(solution)/shard_map/pallas_call | solution.py:483
  138.5 0.7 slice_reduce_fusion
  139.3 0.1 reshape_squeeze.3
  139.4 0.6 reshape.32
  140.0 0.0 copy-start
  140.0 3.3 %copy.16 = f32[128,4096]{1,0:T(8,128)} copy(f32[128,4096]{1,0:T(8,128)} %get-tuple-element.17) | data formatting | bytes 4194304
  143.2 2.3 %copy.17 = f32[64,4096]{1,0:T(8,128)} copy(f32[64,4096]{1,0:T(8,128)} %get-tuple-element.18) | data formatting | bytes 2097152
  145.5 0.0 copy-done
  145.5 2.0 %copy.18 = f32[256,4096]{1,0:T(8,128)} copy(f32[256,4096]{1,0:T(8,128)S(1)} %copy-done) | data formatting | bytes 8388608
  (5 shorter events, 0.1 us)
Async XLA Ops:
  140.0 5.5 %copy-start = (f32[256,4096]{1,0:T(8,128)S(1)}, f32[256,4096]{1,0:T(8,128)}, u32[]{:S(2)}) copy-start(f32[256,4096]{1,0:T(8,128)} %get-tuple-element.19) | copy-start | bytes 12582916

commit v6 on v5

--- a/solution.py
+++ b/solution.py
@@ -10,7 +10,7 @@
 inv_temp = 50.0
 eps = 1e-06
 parts = 4
-ahead = 1
+ahead = 2
 tile = 1024
 strip = 16
 

time: 148 us -> 152 us (1.027)
  Pallas kernels: 135 us -> 139 us
    pallas_call x1, Pallas kernels: 135 us -> 139 us  [local(): pl.pallas_call(functools.partial(kernel, loops, chips, hard_count), out_s...]
where the time goes in v6:
time: 152 us
  Pallas kernels  139 us (91%)
  local copies, waits for them, and re-layouts  10.5 us (7%)
    pallas_call x1, Pallas kernels, local(): pl.pallas_call(functools.partial(kernel, loops, chips, hard_count), out_s...  139 us
    unnamed x5, local copies, waits for them, and re-layouts  7.55 us

profile of v6, /device:TPU:10, one launch (start us, length us, event | category | flops | bytes accessed | tf_op | source)
XLA Modules:
  0.0 151.6 jit_solution(6364112697274055389)
XLA Ops:
  1.3 0.7 concatenate.9
  2.0 0.7 multiply_add_fusion
  2.7 0.1 concatenate.8
  2.9 0.7 tile.10.code_ref
  3.6 139.0 %shard_map.102 = (f32[4,8,128]{2,1,0:T(8,128)}, f32[128,4096]{1,0:T(8,128)}, f32[64,4096]{1,0:T(8,128)}, f32[256,4096]{1,0:T(8,128)}) custom-call(bf16[128,4096]{1,0:T(8,128)(2,1)} %q_ref.1, bf16[64,4096]{1,0:T(8,128)(2,1)} %p_ref.1, bf16[256,4096]{1,0:T(8,128)(2,1)} %n_ref.1, s32[4,8,128]{2,1,0:T(8,128)} %tile.10.code_ref), custom_call_target="tpu_custom_call" | custom-call | tf_op jit(solution)/shard_map/pallas_call | solution.py:483
  142.6 0.7 slice_reduce_fusion
  143.3 0.1 reshape_squeeze.3
  143.4 0.6 reshape.32
  144.0 0.0 copy-start
  144.0 3.3 %copy.16 = f32[128,4096]{1,0:T(8,128)} copy(f32[128,4096]{1,0:T(8,128)} %get-tuple-element.17) | data formatting | bytes 4194304
  147.3 2.3 %copy.17 = f32[64,4096]{1,0:T(8,128)} copy(f32[64,4096]{1,0:T(8,128)} %get-tuple-element.18) | data formatting | bytes 2097152
  149.6 0.0 copy-done
  149.6 2.0 %copy.18 = f32[256,4096]{1,0:T(8,128)} copy(f32[256,4096]{1,0:T(8,128)S(1)} %copy-done) | data formatting | bytes 8388608
  (5 shorter events, 0.1 us)
Async XLA Ops:
  144.0 5.5 %copy-start = (f32[256,4096]{1,0:T(8,128)S(1)}, f32[256,4096]{1,0:T(8,128)}, u32[]{:S(2)}) copy-start(f32[256,4096]{1,0:T(8,128)} %get-tuple-element.19) | copy-start | bytes 12582916
